TPU v7x, 32 devices: a whole 2x2x4 slice. The times are simulated.
32 devices in a mesh: sub: 8 (over y, x, core), slab: 4 (over z).
Axes of the slice: x: 2, y: 2, z: 4, core: 2. Of those that a mesh axis runs over, the one named last changes fastest.
Arguments:
- coarse_basis: bfloat16 [32, 32, 4000], P('sub', 'slab'), may hold values from -6 to 6
- jacobians: bfloat16 [4, 750, 750], replicated, may hold values from -0.21875 to 0.21875
- element_faces: int32 [640, 6], P(('sub', 'slab')), may hold values from 1 to 58, as said below
- element_type: int32 [640], P(('sub', 'slab')), may hold values from 0 to 3
- element_count: int32 [32], P(('sub', 'slab')), may hold values from 1 to 20, 480 in all
- vertex_ids: int32 [32, 32], P(('sub', 'slab')), may hold values from 0 to 31, as said below
Outputs:
- second_image: bfloat16 [32, 32, 4000], P('sub', 'slab')
- coarse_matrix: float32 [32, 32], P('sub')
Inputs may be any that keep to these rules, and one draw needn't show every extreme that they name: `element_faces`: each row names six different cells of the subdomain's extended face grid of (6) x (10) cells, numbered row-major, the own face blocks at rows 1 to 4 and columns 1 to 8; never one of the four corner cells. Each subdomain's live slots are its first element_count slots. `vertex_ids`: the 32 ids of one subdomain are different.
All inputs are finite; a program needn't handle non-finite values. No bound on the sum of `element_count` on one device may be relied on, other than what follows from the above.
Results may differ from a plain program's by a relative error of at most 0.0049.
Values may be sent and summed in bfloat16 or wider, within the bound.
A program may use at most 64 MiB of HBM per device.

v0:
```python
import math

import jax
import jax.numpy as jnp
from jax import lax
from jax.sharding import PartitionSpec as P

CV = 4


def extended_2(x, sides, width):
    for axis, dim in sides:
        peers, length = (lax.axis_size(axis), x.shape[dim])
        up = [(i, (i + 1) % peers) for i in range(peers - 1)]
        down = [(j, i) for i, j in up]
        last = lax.slice_in_dim(x, length - width, length, axis=dim)
        initial = lax.slice_in_dim(x, 0, width, axis=dim)
        before = lax.ppermute(last, axis, up)
        after = lax.ppermute(initial, axis, down)
        x = jnp.concatenate([before, x, after], axis=dim)
    return x


def apply_operator(field, element_faces, element_type, element_count, jacobians):
    row_count = field.shape[0]
    col_count = field.shape[1]
    face_dofs = jacobians.shape[1] // 6
    columns = field.shape[2] // face_dofs
    extended = extended_2(field, (("sub", 0), ("slab", 1)), 1)
    flat_faces = extended.reshape(-1, face_dofs, columns)
    slot_count = element_faces.shape[0]

    def visit(slot_index, totals):
        picked = lax.dynamic_index_in_dim(element_faces, slot_index, 0, keepdims=False)
        element_kind = lax.dynamic_index_in_dim(element_type, slot_index, 0, keepdims=False)
        face_block = jnp.take(flat_faces, picked, axis=0).reshape(6 * face_dofs, columns)
        matrix = lax.dynamic_index_in_dim(jacobians, element_kind, 0, keepdims=False)
        product = jnp.dot(matrix, face_block, preferred_element_type=jnp.float32).reshape(
            6, face_dofs, columns
        )
        weight = (slot_index < element_count[0]).astype(jnp.float32)
        return totals.at[picked].add(product * weight)

    start_totals = jnp.zeros((flat_faces.shape[0], face_dofs, columns), jnp.float32)
    totals = lax.fori_loop(0, slot_count, visit, start_totals)
    gathered = totals.reshape(row_count + 2, col_count + 2, face_dofs * columns)
    returned = extended_2(gathered, (("sub", 0), ("slab", 1)), 1)
    owned = gathered[1:-1, 1:-1]
    owned = owned.at[0].add(returned[0, 2 : col_count + 2])
    owned = owned.at[row_count - 1].add(returned[row_count + 3, 2 : col_count + 2])
    owned = owned.at[:, 0].add(returned[2 : row_count + 2, 0])
    owned = owned.at[:, col_count - 1].add(returned[2 : row_count + 2, col_count + 3])
    return owned


def body(coarse_basis, jacobians, element_faces, element_type, element_count, vertex_ids):
    first_image = apply_operator(
        coarse_basis, element_faces, element_type, element_count, jacobians
    ).astype(jnp.bfloat16)
    second_image = apply_operator(
        first_image, element_faces, element_type, element_count, jacobians
    ).astype(jnp.bfloat16)
    face_dofs = jacobians.shape[1] // 6
    columns = coarse_basis.shape[2] // face_dofs
    left_basis = coarse_basis.reshape(-1, columns)
    right_image = first_image.reshape(-1, columns)
    local_coarse = lax.dot_general(
        left_basis, right_image, (((0,), (0,)), ((), ())), preferred_element_type=jnp.float32
    )
    local_coarse = local_coarse * (1.0 / math.sqrt(left_basis.shape[0]))
    vertex_total = CV * lax.axis_size("sub")
    one_hot = (vertex_ids[0][:, None] == jnp.arange(vertex_total, dtype=jnp.int32)[None, :]).astype(
        jnp.float32
    )
    placed = jnp.dot(
        local_coarse, one_hot, precision=lax.Precision.HIGHEST, preferred_element_type=jnp.float32
    )
    dense_terms = jnp.dot(
        one_hot.T, placed, precision=lax.Precision.HIGHEST, preferred_element_type=jnp.float32
    )
    row_part = lax.psum_scatter(dense_terms, "sub", scatter_dimension=0, tiled=True)
    coarse_matrix = lax.psum(row_part, "slab")
    return (second_image, coarse_matrix)


def solution(mesh):
    return jax.shard_map(
        body,
        mesh=mesh,
        in_specs=(
            P("sub", "slab", None),
            P(),
            P(("sub", "slab"), None),
            P(("sub", "slab")),
            P(("sub", "slab")),
            P(("sub", "slab"), None),
        ),
        out_specs=(P("sub", "slab", None), P("sub", None)),
        check_vma=False,
    )
```

profile of v0, /device:TPU:1, one launch (start us, length us, event | category | flops | bytes accessed | tf_op | source)
XLA Modules:
  0.0 525.0 jit_solution(13425476581707076553)
XLA Ops:
  1.5 4.5 collective-permute-start
  9.0 2.7 collective-permute-done.1
  11.8 3.2 collective-permute-start.2
  16.3 5.0 copy.39
  21.8 2.7 reshape.341
  24.6 178.0 %while.34 = (s32[]{:T(128)}, f32[60,125,32]{1,2,0:T(8,128)S(1)}, s32[20,6]{1,0:T(8,128)S(1)}, s32[20]{0:T(128)S(1)}, bf16[4,750,750]{2,1,0:T(8,128)(2,1)}, /*ind...) while((s32[]{:T(128)}, f32[60,125,32]{1,2,0:T(8,128)S(1)}, ...), condition=%wide.region_2.4_spmd, body=%wide.region_0.3_spmd.sunk | while | flops 36073084 | bytes 6445453 | solution.py:45
  208.6 2.7 copy.35
  211.3 3.2 reshape.342
  220.1 6.1 %collective-permute-done.5 = f32[1,10,4000]{2,1,0:T(8,128)S(1)} collective-permute-done((f32[1,10,4000]{2,1,0:T(8,128)}, f32[1,10,4000]{2,1,0:T(8,128)S(1)}, u32[]{:S(2)}, u32[]{:S(2)}) %collective-permute-start.5) | collective-permute-done | bytes 160032 | tf_op jit(solution)/shard_map/ppermute | solution.py:19
  226.4 4.0 collective-permute-start.6
  232.8 3.5 collective-permute-done.7
  238.5 3.3 collective-permute-start.8
  244.1 3.3 collective-permute-done.9
  247.6 3.2 collective-permute-start.10
  252.5 3.6 collective-permute-done.11
  256.5 2.7 reshape.343
  259.3 204.7 %while.35 = (s32[]{:T(128)}, f32[60,125,32]{1,2,0:T(8,128)S(1)}, s32[20,6]{1,0:T(8,128)}, s32[20]{0:T(128)S(1)}, bf16[4,750,750]{2,1,0:T(8,128)(2,1)}, /*index=5...) while((s32[]{:T(128)}, f32[60,125,32]{1,2,0:T(8,128)S(1)}, ...), condition=%wide.region_5.7_spmd, body=%wide.region_3.6_spmd.sunk | while | flops 36073084 | bytes 6445453 | solution.py:45
  464.6 3.5 collective-permute-start.12
  468.4 22.2 %all-reduce = f32[32,32]{1,0:T(8,128)S(1)} all-reduce(f32[32,32]{1,0:T(8,128)S(1)} %fusion.6), channel_id=2, replica_groups=mesh['sub'=8,'slab'=4] {'sub'}, use_global_device_ids=true, to_apply=%region_6.8.clone | all-reduce | flops 1024 | bytes 8192
  490.6 8.5 %psum.7 = f32[4,32]{1,0:T(4,128)} all-reduce(f32[4,32]{1,0:T(4,128)S(1)} %constant_dynamic-slice_fusion.4), channel_id=1, replica_groups=mesh['sub'=8,'slab'=4] {'slab'}, use_global_device_ids=true, to_apply=%region_7.9 | all-reduce | flops 128 | bytes 1024 | tf_op jit(solution)/shard_map/psum | solution.py:82
  501.7 3.2 reshape.344
  505.5 5.3 %collective-permute-start.13 = (f32[1,10,4000]{2,1,0:T(8,128)S(1)}, f32[1,10,4000]{2,1,0:T(8,128)S(1)}, u32[]{:S(2)}, u32[]{:S(2)}) collective-permute-start(f32[1,10,4000]{2,1,0:T(8,128)S(1)} %slice.298), channel_id=1, source_target_pairs={{4,0},{8,4},{12,8},{16,12},{20,16},{24,20},{28,24},{5,1},{9,5},{13... | collective-permute-start | bytes 480008 | tf_op jit(solution)/shard_map/ppermute | solution.py:19
  511.1 4.8 collective-permute-done.13
  520.4 3.3 collective-permute-done.15
  (564 shorter events, 312.2 us)
Async XLA Ops:
  1.5 6.4 %collective-permute-start = (bf16[1,8,4000]{2,1,0:T(8,128)(2,1)S(1)}, bf16[1,8,4000]{2,1,0:T(8,128)(2,1)S(1)}, u32[]{:S(2)}, u32[]{:S(2)}) collective-permute-start(bf16[1,8,4000]{2,1,0:T(8,128)(2,1)S(1)} %get-tuple-element.438), channel_id=1, source_target_pairs={{0,4},{4,8},{8,12},{12,16},{16,20},{20,24},{24,28},{1,5},{5,9},{9,... | collective-permute-start | bytes 192008 | tf_op jit(solution)/shard_map/ppermute | solution.py:18
  6.0 5.6 %collective-permute-start.1 = (bf16[1,8,4000]{2,1,0:T(8,128)(2,1)S(1)}, bf16[1,8,4000]{2,1,0:T(8,128)(2,1)S(1)}, u32[]{:S(2)}, u32[]{:S(2)}) collective-permute-start(bf16[1,8,4000]{2,1,0:T(8,128)(2,1)S(1)} %get-tuple-element.437), channel_id=1, source_target_pairs={{4,0},{8,4},{12,8},{16,12},{20,16},{24,20},{28,24},{5,1},{9,5},{13... | collective-permute-start | bytes 192008 | tf_op jit(solution)/shard_map/ppermute | solution.py:19
  11.8 9.6 %collective-permute-start.2 = (bf16[6,1,4000]{2,1,0:T(2,128)(2,1)S(1)}, bf16[6,1,4000]{2,1,0:T(2,128)(2,1)S(1)}, u32[]{:S(2)}, u32[]{:S(2)}) collective-permute-start(bf16[6,1,4000]{2,1,0:T(2,128)(2,1)S(1)} %get-tuple-element.433), channel_id=1, source_target_pairs={{0,1},{1,2},{2,3},{4,5},{5,6},{6,7},{8,9},{9,10},{10,11},{12,13},{... | collective-permute-start | bytes 144008 | tf_op jit(solution)/shard_map/ppermute | solution.py:18
  15.0 6.3 %copy-start.2 = (s32[20,6]{0,1:T(8,128)S(1)}, s32[20,6]{0,1:T(8,128)}, u32[]{:S(2)}) copy-start(s32[20,6]{0,1:T(8,128)} %param.30) | copy-start | bytes 1444
  15.0 6.4 %collective-permute-start.3 = (bf16[6,1,4000]{2,1,0:T(2,128)(2,1)S(1)}, bf16[6,1,4000]{2,1,0:T(2,128)(2,1)S(1)}, u32[]{:S(2)}, u32[]{:S(2)}) collective-permute-start(bf16[6,1,4000]{2,1,0:T(2,128)(2,1)S(1)} %get-tuple-element.434), channel_id=1, source_target_pairs={{1,0},{2,1},{3,2},{5,4},{6,5},{7,6},{9,8},{10,9},{11,10},{13,12},{... | collective-permute-start | bytes 144008 | tf_op jit(solution)/shard_map/ppermute | solution.py:19
  21.8 2.8 copy-start.3
  202.6 0.6 copy-start.1
  202.6 3.8 copy-start
  202.6 4.7 copy-start.5
  204.2 15.8 %collective-permute-start.4 = (f32[1,10,4000]{2,1,0:T(8,128)}, f32[1,10,4000]{2,1,0:T(8,128)S(1)}, u32[]{:S(2)}, u32[]{:S(2)}) collective-permute-start(f32[1,10,4000]{2,1,0:T(8,128)} %slice.275), channel_id=1, source_target_pairs={{0,4},{4,8},{8,12},{12,16},{16,20},{20,24},{24,28},{1,5},{5,9},{9,... | collective-permute-start | bytes 480008 | tf_op jit(solution)/shard_map/ppermute | solution.py:18
  217.9 8.3 %collective-permute-start.5 = (f32[1,10,4000]{2,1,0:T(8,128)}, f32[1,10,4000]{2,1,0:T(8,128)S(1)}, u32[]{:S(2)}, u32[]{:S(2)}) collective-permute-start(f32[1,10,4000]{2,1,0:T(8,128)} %slice.279), channel_id=1, source_target_pairs={{4,0},{8,4},{12,8},{16,12},{20,16},{24,20},{28,24},{5,1},{9,5},{13... | collective-permute-start | bytes 480008 | tf_op jit(solution)/shard_map/ppermute | solution.py:19
  226.4 5.9 %collective-permute-start.6 = (f32[8,1,4000]{2,1,0:T(1,128)S(1)}, f32[8,1,4000]{2,1,0:T(1,128)S(1)}, u32[]{:S(2)}, u32[]{:S(2)}) collective-permute-start(f32[8,1,4000]{2,1,0:T(1,128)S(1)} %get-tuple-element.426), channel_id=1, source_target_pairs={{0,1},{1,2},{2,3},{4,5},{5,6},{6,7},{8,9},{9,10},{10,11},{12,13},{... | collective-permute-start | bytes 384008 | tf_op jit(solution)/shard_map/ppermute | solution.py:18
  230.4 5.8 %collective-permute-start.7 = (f32[8,1,4000]{2,1,0:T(1,128)S(1)}, f32[8,1,4000]{2,1,0:T(1,128)}, u32[]{:S(2)}, u32[]{:S(2)}) collective-permute-start(f32[8,1,4000]{2,1,0:T(1,128)S(1)} %get-tuple-element.425), channel_id=1, source_target_pairs={{1,0},{2,1},{3,2},{5,4},{6,5},{7,6},{9,8},{10,9},{11,10},{13,12},{... | collective-permute-start | bytes 384008 | tf_op jit(solution)/shard_map/ppermute | solution.py:19
  238.5 13.8 %copy-start.4 = (s32[1,32]{1,0:T(1,128)S(1)}, s32[1,32]{1,0:T(1,128)}, u32[]{:S(2)}) copy-start(s32[1,32]{1,0:T(1,128)} %param.33) | copy-start | bytes 388
  238.5 5.6 %collective-permute-start.8 = (bf16[1,8,4000]{2,1,0:T(8,128)(2,1)S(1)}, bf16[1,8,4000]{2,1,0:T(8,128)(2,1)S(1)}, u32[]{:S(2)}, u32[]{:S(2)}) collective-permute-start(bf16[1,8,4000]{2,1,0:T(8,128)(2,1)S(1)} %get-tuple-element.435), channel_id=1, source_target_pairs={{0,4},{4,8},{8,12},{12,16},{16,20},{20,24},{24,28},{1,5},{5,9},{9,... | collective-permute-start | bytes 192008 | tf_op jit(solution)/shard_map/ppermute | solution.py:18
  241.8 5.6 %collective-permute-start.9 = (bf16[1,8,4000]{2,1,0:T(8,128)(2,1)S(1)}, bf16[1,8,4000]{2,1,0:T(8,128)(2,1)S(1)}, u32[]{:S(2)}, u32[]{:S(2)}) collective-permute-start(bf16[1,8,4000]{2,1,0:T(8,128)(2,1)S(1)} %get-tuple-element.436), channel_id=1, source_target_pairs={{4,0},{8,4},{12,8},{16,12},{20,16},{24,20},{28,24},{5,1},{9,5},{13... | collective-permute-start | bytes 192008 | tf_op jit(solution)/shard_map/ppermute | solution.py:19
  247.6 4.9 collective-permute-start.10
  250.8 5.4 %collective-permute-start.11 = (bf16[6,1,4000]{2,1,0:T(2,128)(2,1)S(1)}, bf16[6,1,4000]{2,1,0:T(2,128)(2,1)S(1)}, u32[]{:S(2)}, u32[]{:S(2)}) collective-permute-start(bf16[6,1,4000]{2,1,0:T(2,128)(2,1)S(1)} %get-tuple-element.432), channel_id=1, source_target_pairs={{1,0},{2,1},{3,2},{5,4},{6,5},{7,6},{9,8},{10,9},{11,10},{13,12},{... | collective-permute-start | bytes 144008 | tf_op jit(solution)/shard_map/ppermute | solution.py:19
  464.6 46.3 %collective-permute-start.12 = (f32[1,10,4000]{2,1,0:T(8,128)S(1)}, f32[1,10,4000]{2,1,0:T(8,128)S(1)}, u32[]{:S(2)}, u32[]{:S(2)}) collective-permute-start(f32[1,10,4000]{2,1,0:T(8,128)S(1)} %slice.294), channel_id=1, source_target_pairs={{0,4},{4,8},{8,12},{12,16},{16,20},{20,24},{24,28},{1,5},{5,9},{9,... | collective-permute-start | bytes 480008 | tf_op jit(solution)/shard_map/ppermute | solution.py:18
  505.5 10.3 %collective-permute-start.13 = (f32[1,10,4000]{2,1,0:T(8,128)S(1)}, f32[1,10,4000]{2,1,0:T(8,128)S(1)}, u32[]{:S(2)}, u32[]{:S(2)}) collective-permute-start(f32[1,10,4000]{2,1,0:T(8,128)S(1)} %slice.298), channel_id=1, source_target_pairs={{4,0},{8,4},{12,8},{16,12},{20,16},{24,20},{28,24},{5,1},{9,5},{13... | collective-permute-start | bytes 480008 | tf_op jit(solution)/shard_map/ppermute | solution.py:19
  516.1 3.9 collective-permute-start.14
  518.1 5.7 %collective-permute-start.15 = (f32[8,1,4000]{2,1,0:T(1,128)S(1)}, f32[8,1,4000]{2,1,0:T(1,128)S(1)}, u32[]{:S(2)}, u32[]{:S(2)}) collective-permute-start(f32[8,1,4000]{2,1,0:T(1,128)S(1)} %get-tuple-element.423), channel_id=1, source_target_pairs={{1,0},{2,1},{3,2},{5,4},{6,5},{7,6},{9,8},{10,9},{11,10},{13,12},{... | collective-permute-start | bytes 384008 | tf_op jit(solution)/shard_map/ppermute | solution.py:19
where the time goes:
time: 533 us; the launch traced here: 525 us
  local copies, waits for them, and re-layouts  229 us (43%)
  loops' own time  107 us (20%)
  other arithmetic  66.2 us (12%)
  starting transfers between devices  42.5 us (8%)
  blocking collectives  30.7 us (6%)
  waiting for transfers between devices  28.3 us (5%)
  matrix products  19.7 us (4%)
    another operation x2, loops' own time, apply_operator(): totals = lax.fori_loop(0, slot_count, visit, start_totals)  107 us
    gather x40, local copies, waits for them, and re-layouts, visit(): jnp.take(flat_faces, picked, axis=0).reshape(6 * face_dofs, columns)  85.2 us
    dynamic_slice x40, local copies, waits for them, and re-layouts, visit(): lax.dynamic_index_in_dim(jacobians, element_kind, 0, keepdims=False)  53.6 us
    scatter-add x40, other arithmetic, visit(): return totals.at[picked].add(product * weight)  30.7 us
    ppermute x8, waiting for transfers between devices, extended_2(): after = lax.ppermute(initial, axis, down)  27.2 us
    ppermute x8, starting transfers between devices, extended_2(): before = lax.ppermute(last, axis, up)  25.9 us
    dynamic_slice x40, local copies, waits for them, and re-layouts, visit(): lax.dynamic_index_in_dim(element_type, slot_index, 0, keepdims=False)  23.5 us
    unnamed x1, blocking collectives  22.2 us
  transfers between devices with their start and end apart: 16, of which 9 were waited for; matrix products, arithmetic and copies ran while one was open for 5% of the time, Pallas kernels for 0%

commit v1 on v0

v1 whole, which is shorter than its diff:
```python
import functools
import math

import jax
import jax.numpy as jnp
from jax import lax
from jax.experimental import pallas as pl
from jax.experimental.pallas import tpu as pltpu
from jax.sharding import PartitionSpec as P

FX = 4
FY = 8
EX = FX + 2
EY = FY + 2
CELLS = EX * EY
CV = 4
LANES = 128
GROUP = 4
MESH = pl.DeviceIdType.MESH
NT = (((1,), (1,)), ((), ()))


def cell(r, c):
    return r * EY + c


def kernel(
    subs, slabs, slots, dofs,
    x_ref, jac_hbm, meta_ref, ids_ref,
    out_ref, coarse_ref,
    field, jac, pieces, totals, sent, sent_cols, sent_diag, sent_cols_2,
    rim_cols, got_rows, got_cols, got_diag, got_rows_2, got_cols_2,
    dense, got_dense, row_sum, got_sum,
    jac_sem, s0, r0, s1, r1, s2, r2, cs1, cr1, cs2, cr2,
):
    i = lax.axis_index("sub")
    j = lax.axis_index("slab")
    up, down, left, right = i > 0, i < subs - 1, j > 0, j < slabs - 1
    columns = x_ref.shape[1]
    f32 = jnp.float32
    bf16 = jnp.bfloat16

    jac_copy = pltpu.make_async_copy(jac_hbm, jac, jac_sem)
    jac_copy.start()

    barrier = pltpu.get_barrier_semaphore()

    def greet(di, dj):
        pl.semaphore_signal(barrier, inc=1, device_id={"sub": di, "slab": dj}, device_id_type=MESH)

    diagonals = (
        (jnp.logical_and(down, right), i + 1, j + 1),
        (jnp.logical_and(down, left), i + 1, j - 1),
        (jnp.logical_and(up, right), i - 1, j + 1),
        (jnp.logical_and(up, left), i - 1, j - 1),
    )
    from_diagonals = tuple(diagonals[3 - k][0] for k in range(4))

    @pl.loop(1, subs)
    def _(k):
        greet(lax.rem(i + k, subs), j)

    @pl.loop(1, slabs)
    def _(k):
        greet(i, lax.rem(j + k, slabs))

    for there, di, dj in diagonals:
        @pl.when(there)
        def _():
            greet(di, dj)

    @pl.loop(0, pieces.shape[0])
    def _(k):
        pieces[k] = jnp.zeros(pieces.shape[1:], f32)

    blank = jnp.zeros((columns, LANES), bf16)
    for c in (cell(0, 0), cell(0, EY - 1), cell(EX - 1, 0), cell(EX - 1, EY - 1)):
        field[c] = blank

    def fill(there, ref):
        @pl.when(jnp.logical_not(there))
        def _():
            ref[...] = jnp.zeros(ref.shape, ref.dtype)

    sides = (up, down, left, right)
    fill(up, field.at[pl.ds(cell(0, 1), FY)])
    fill(down, field.at[pl.ds(cell(EX - 1, 1), FY)])
    fill(left, rim_cols.at[0])
    fill(right, rim_cols.at[1])
    fill(up, got_rows.at[0])
    fill(down, got_rows.at[1])
    fill(left, got_cols.at[0])
    fill(right, got_cols.at[1])
    fill(up, got_rows_2.at[0])
    fill(down, got_rows_2.at[1])
    fill(left, got_cols_2.at[0])
    fill(right, got_cols_2.at[1])
    for k in range(4):
        fill(from_diagonals[k], got_diag.at[k])

    for r in range(FX):
        for c in range(FY):
            field[cell(r + 1, c + 1)] = x_ref[r * FY + c]

    vertical = up.astype(jnp.int32) + down.astype(jnp.int32)
    sideways = left.astype(jnp.int32) + right.astype(jnp.int32)
    pl.semaphore_wait(barrier, subs - 1 + slabs - 1 + vertical * sideways)

    def remote(src, dst, send, recv, di, dj):
        return pltpu.make_async_remote_copy(
            src_ref=src, dst_ref=dst, send_sem=send, recv_sem=recv,
            device_id={"sub": di, "slab": dj}, device_id_type=MESH,
        )

    def exchange(copies):
        for there, coming, copy in copies:
            @pl.when(there)
            def _():
                copy.start()

    def arrive(copies):
        for there, coming, copy in copies:
            @pl.when(coming)
            def _():
                copy.wait_recv()

    def leave(copies):
        for there, coming, copy in copies:
            @pl.when(there)
            def _():
                copy.wait_send()

    x_cols = x_ref.reshape(FX, FY, columns, LANES)
    first = (
        (up, down, remote(x_ref.at[pl.ds(0, FY)], field.at[pl.ds(cell(EX - 1, 1), FY)],
                          s0.at[0], r0.at[0], i - 1, j)),
        (down, up, remote(x_ref.at[pl.ds((FX - 1) * FY, FY)], field.at[pl.ds(cell(0, 1), FY)],
                          s0.at[1], r0.at[1], i + 1, j)),
        (left, right, remote(x_cols.at[:, 0], rim_cols.at[1], s0.at[2], r0.at[2], i, j - 1)),
        (right, left, remote(x_cols.at[:, FY - 1], rim_cols.at[0], s0.at[3], r0.at[3], i, j + 1)),
    )
    exchange(first)
    jac_copy.wait()
    arrive(first)
    for r in range(FX):
        field[cell(r + 1, 0)] = rim_cols[0, r]
        field[cell(r + 1, EY - 1)] = rim_cols[1, r]

    def apply():
        @pl.loop(0, slots // GROUP)
        def _(g):
            for k in range(GROUP):
                e = g * GROUP + k
                x = jnp.concatenate(
                    [field[meta_ref[e * 6 + p]][:, :dofs] for p in range(6)], axis=1
                )
                y = lax.dot_general(
                    x, jac[meta_ref[slots * 6 + e]], NT, preferred_element_type=f32
                )
                for p in range(6):
                    pieces[1 + e * 6 + p, :, :dofs] = y[:, p * dofs : (p + 1) * dofs]

        @pl.loop(0, CELLS)
        def _(c):
            base = slots * 7 + c * slots
            total = pieces[meta_ref[base]]
            for e in range(1, slots):
                total = total + pieces[meta_ref[base + e]]
            totals[c] = total
            sent[c] = total.astype(bf16)

    apply()
    for r in range(FX):
        for k in range(2):
            sent_cols[0, r, k] = sent[cell(r + 1, k)]
            sent_cols[1, r, k] = sent[cell(r + 1, FY + k)]
    corners = (
        (cell(FX, EY - 1), cell(EX - 1, FY)),
        (cell(FX, 0), cell(EX - 1, 1)),
        (cell(1, EY - 1), cell(0, FY)),
        (cell(1, 0), cell(0, 1)),
    )
    for k in range(4):
        for n in range(2):
            sent_diag[k, n] = sent[corners[k][n]]
    span = EY + FY
    second = (
        (up, down, remote(sent.at[pl.ds(cell(0, 1), span)], got_rows.at[1],
                          s1.at[0], r1.at[0], i - 1, j)),
        (down, up, remote(sent.at[pl.ds(cell(FX, 1), span)], got_rows.at[0],
                          s1.at[1], r1.at[1], i + 1, j)),
        (left, right, remote(sent_cols.at[0], got_cols.at[1], s1.at[2], r1.at[2], i, j - 1)),
        (right, left, remote(sent_cols.at[1], got_cols.at[0], s1.at[3], r1.at[3], i, j + 1)),
    ) + tuple(
        (diagonals[k][0], from_diagonals[k],
         remote(sent_diag.at[k], got_diag.at[k], s1.at[4 + k], r1.at[4 + k],
                diagonals[k][1], diagonals[k][2]))
        for k in range(4)
    )
    exchange(second)
    leave(first)
    arrive(second)

    def wide(ref, *at):
        return ref[at].astype(f32)

    for r in range(1, FX + 1):
        for c in range(1, FY + 1):
            v = totals[cell(r, c)]
            if r == 1:
                v = v + wide(got_rows, 0, EY + c - 1)
            if r == FX:
                v = v + wide(got_rows, 1, c - 1)
            if c == 1:
                v = v + wide(got_cols, 0, r - 1, 1)
            if c == FY:
                v = v + wide(got_cols, 1, r - 1, 0)
            field[cell(r, c)] = v.astype(bf16)

    def keep(there, c, v):
        field[c] = jnp.where(there, v, 0.0).astype(bf16)

    for c in range(1, FY + 1):
        v = totals[cell(0, c)] + wide(got_rows, 0, c - 1)
        w = totals[cell(EX - 1, c)] + wide(got_rows, 1, EY + c - 1)
        if c == 1:
            v, w = v + wide(got_diag, 0, 0), w + wide(got_diag, 2, 0)
        if c == FY:
            v, w = v + wide(got_diag, 1, 0), w + wide(got_diag, 3, 0)
        keep(up, cell(0, c), v)
        keep(down, cell(EX - 1, c), w)
    for r in range(1, FX + 1):
        v = totals[cell(r, 0)] + wide(got_cols, 0, r - 1, 0)
        w = totals[cell(r, EY - 1)] + wide(got_cols, 1, r - 1, 1)
        if r == 1:
            v, w = v + wide(got_diag, 0, 1), w + wide(got_diag, 1, 1)
        if r == FX:
            v, w = v + wide(got_diag, 2, 1), w + wide(got_diag, 3, 1)
        keep(left, cell(r, 0), v)
        keep(right, cell(r, EY - 1), w)

    local = jnp.zeros((columns, columns), f32)
    for r in range(FX):
        for c in range(FY):
            local = local + lax.dot_general(
                x_ref[r * FY + c], field[cell(r + 1, c + 1)], NT, preferred_element_type=f32
            )
    local = local * (1.0 / math.sqrt(FX * FY * dofs))
    ids = ids_ref[...]
    width = dense.shape[1]
    spots = lax.broadcasted_iota(jnp.int32, (width, columns), 0)
    one_hot = jnp.where(spots == ids, 1.0, 0.0).astype(f32)
    rows = lax.broadcasted_iota(jnp.int32, (8 * subs, columns), 0)
    spot = jnp.where(rows % 8 < CV, rows // 8 * CV + rows % 8, -1)
    row_hot = jnp.where(spot == ids, 1.0, 0.0).astype(f32)
    placed = lax.dot_general(
        local, one_hot, NT, precision=lax.Precision.HIGHEST, preferred_element_type=f32
    )
    dense[...] = jnp.dot(
        row_hot, placed, precision=lax.Precision.HIGHEST, preferred_element_type=f32
    )

    def block(s):
        return dense.at[pl.ds(pl.multiple_of(s * 8, 8), 8)]

    def to_sub(s):
        return remote(block(s), got_dense.at[i], cs1.at[s], cr1.at[i], s, j)

    def from_sub(s):
        return remote(block(s), got_dense.at[s], cs1.at[s], cr1.at[s], s, j)

    def to_slab(s):
        return remote(row_sum, got_sum.at[j], cs2.at[s], cr2.at[j], i, s)

    def from_slab(s):
        return remote(row_sum, got_sum.at[s], cs2.at[s], cr2.at[s], i, s)

    @pl.loop(1, subs)
    def _(k):
        to_sub(lax.rem(i + k, subs)).start()

    leave(second)
    apply()

    for r in range(FX):
        sent_cols_2[0, r] = sent[cell(r + 1, 0)]
        sent_cols_2[1, r] = sent[cell(r + 1, EY - 1)]
    third = (
        (up, down, remote(sent.at[pl.ds(cell(0, 1), FY)], got_rows_2.at[1],
                          s2.at[0], r2.at[0], i - 1, j)),
        (down, up, remote(sent.at[pl.ds(cell(EX - 1, 1), FY)], got_rows_2.at[0],
                          s2.at[1], r2.at[1], i + 1, j)),
        (left, right, remote(sent_cols_2.at[0], got_cols_2.at[1], s2.at[2], r2.at[2], i, j - 1)),
        (right, left, remote(sent_cols_2.at[1], got_cols_2.at[0], s2.at[3], r2.at[3], i, j + 1)),
    )
    exchange(third)

    row_sum[...] = block(i)[...]

    @pl.loop(1, subs)
    def _(k):
        s = lax.rem(i + k, subs)
        from_sub(s).wait_recv()
        row_sum[...] += got_dense[s]

    @pl.loop(1, slabs)
    def _(k):
        to_slab(lax.rem(j + k, slabs)).start()

    arrive(third)
    for r in range(1, FX + 1):
        for c in range(1, FY + 1):
            v = totals[cell(r, c)]
            if r == 1:
                v = v + wide(got_rows_2, 0, c - 1)
            if r == FX:
                v = v + wide(got_rows_2, 1, c - 1)
            if c == 1:
                v = v + wide(got_cols_2, 0, r - 1)
            if c == FY:
                v = v + wide(got_cols_2, 1, r - 1)
            out_ref[(r - 1) * FY + c - 1] = v.astype(bf16)

    coarse_ref[...] = row_sum[...]

    @pl.loop(1, slabs)
    def _(k):
        s = lax.rem(j + k, slabs)
        from_slab(s).wait_recv()
        coarse_ref[...] += got_sum[s]

    leave(third)

    @pl.loop(1, subs)
    def _(k):
        to_sub(lax.rem(i + k, subs)).wait_send()

    @pl.loop(1, slabs)
    def _(k):
        to_slab(lax.rem(j + k, slabs)).wait_send()


def body(coarse_basis, jacobians, element_faces, element_type, element_count, vertex_ids):
    subs, slabs = lax.axis_size("sub"), lax.axis_size("slab")
    dofs = jacobians.shape[1] // 6
    columns = coarse_basis.shape[2] // dofs
    slots = element_faces.shape[0]
    vertex_total = CV * subs
    width = -(-vertex_total // LANES) * LANES
    f32, bf16 = jnp.float32, jnp.bfloat16

    x = coarse_basis.reshape(FX * FY, dofs, columns).transpose(0, 2, 1)
    x = jnp.pad(x, ((0, 0), (0, 0), (0, LANES - dofs)))
    slot = jnp.arange(slots, dtype=jnp.int32)
    which = slot[:, None] * 6 + jnp.arange(1, 7, dtype=jnp.int32)[None, :]
    which = jnp.where((slot < element_count[0])[:, None], which, 0)
    cells = jnp.arange(CELLS, dtype=jnp.int32)
    inverse = jnp.sum(
        jnp.where(element_faces[None] == cells[:, None, None], which[None], 0), axis=2
    )
    meta = jnp.concatenate([element_faces.reshape(-1), element_type, inverse.reshape(-1)])

    def block(*lead):
        return pltpu.VMEM((*lead, columns, LANES), bf16)

    vmem = pl.BlockSpec(memory_space=pltpu.VMEM)
    dma = pltpu.SemaphoreType.DMA
    out, coarse = pl.pallas_call(
        functools.partial(kernel, subs, slabs, slots, dofs),
        out_shape=(
            jax.ShapeDtypeStruct((FX * FY, columns, LANES), bf16),
            jax.ShapeDtypeStruct((8, width), f32),
        ),
        in_specs=[
            vmem,
            pl.BlockSpec(memory_space=pl.ANY),
            pl.BlockSpec(memory_space=pltpu.SMEM),
            vmem,
        ],
        out_specs=(vmem, vmem),
        scratch_shapes=[
            block(CELLS),
            pltpu.VMEM(jacobians.shape, bf16),
            pltpu.VMEM((1 + 6 * slots, columns, LANES), f32),
            pltpu.VMEM((CELLS, columns, LANES), f32),
            block(CELLS),
            block(2, FX, 2),
            block(4, 2),
            block(2, FX),
            block(2, FX),
            block(2, EY + FY),
            block(2, FX, 2),
            block(4, 2),
            block(2, FY),
            block(2, FX),
            pltpu.VMEM((8 * subs, width), f32),
            pltpu.VMEM((subs, 8, width), f32),
            pltpu.VMEM((8, width), f32),
            pltpu.VMEM((slabs, 8, width), f32),
            dma,
            dma((4,)), dma((4,)),
            dma((8,)), dma((8,)),
            dma((4,)), dma((4,)),
            dma((subs,)), dma((subs,)),
            dma((slabs,)), dma((slabs,)),
        ],
        compiler_params=pltpu.CompilerParams(
            collective_id=0, has_side_effects=True, vmem_limit_bytes=40 * 1024 * 1024
        ),
        cost_estimate=pl.CostEstimate(
            flops=4 * slots * (6 * dofs) ** 2 * columns,
            bytes_accessed=2 * jacobians.size,
            transcendentals=0,
        ),
    )(x, jacobians, meta, vertex_ids)
    out = out[:, :, :dofs].transpose(0, 2, 1).reshape(FX, FY, dofs * columns)
    return out, coarse[:CV, :vertex_total]


def solution(mesh):
    return jax.shard_map(
        body,
        mesh=mesh,
        in_specs=(
            P("sub", "slab", None),
            P(),
            P(("sub", "slab"), None),
            P(("sub", "slab")),
            P(("sub", "slab")),
            P(("sub", "slab"), None),
        ),
        out_specs=(P("sub", "slab", None), P("sub", None)),
        check_vma=False,
    )
```

time: 533 us -> 50.5 us (0.09); the launches traced: 525 us -> 50.2 us
  local copies, waits for them, and re-layouts: 229 us -> 9.94 us
  loops' own time: 107 us -> 0 us
  other arithmetic: 66.2 us -> 0.88 us
  starting transfers between devices: 42.5 us -> 0 us
  Pallas kernels: 0 us -> 38 us
  blocking collectives: 30.7 us -> 0 us
  waiting for transfers between devices: 28.3 us -> 0 us
  matrix products: 19.7 us -> 0 us
    another operation x2 -> x0, loops' own time: 107 us -> none  [apply_operator(): totals = lax.fori_loop(0, slot_count, visit, start_totals)]
    gather x40 -> x0, local copies, waits for them, and re-layouts: 85.2 us -> none  [visit(): jnp.take(flat_faces, picked, axis=0).reshape(6 * face_dofs, columns)]
    dynamic_slice x80 -> x0, local copies, waits for them, and re-layouts: 77.1 us -> none  [the longest x40 53.6 us: visit(): lax.dynamic_index_in_dim(jacobians, element_kind, 0, keepdims=False)]
    ppermute x16 -> x0, starting transfers between devices: 42.5 us -> none  [the longest x8 25.9 us: extended_2(): before = lax.ppermute(last, axis, up)]
    pallas_call x0 -> x1, Pallas kernels: none -> 38 us  [body(): pl.pallas_call(functools.partial(kernel, subs, slabs, slots, dofs), out_s...]
    scatter-add x44 -> x0, other arithmetic: 30.9 us -> none  [the longest x40 30.7 us: visit(): return totals.at[picked].add(product * weight)]
    ppermute x16 -> x0, waiting for transfers between devices: 28.3 us -> none  [the longest x8 27.2 us: extended_2(): after = lax.ppermute(initial, axis, down)]
    unnamed x1 -> x0, blocking collectives: 22.2 us -> none
  transfers between devices with their start and end apart: 16 -> 0, of which waited for: 9 -> 0; matrix products, arithmetic and copies ran while one was open for 5% -> 0% of each run, Pallas kernels for 0% -> 0%
where the time goes in v1:
time: 50.5 us; the launch traced here: 50.2 us
  Pallas kernels  38 us (75%)
  local copies, waits for them, and re-layouts  9.94 us (20%)
  between operations  1.37 us (3%)
  other arithmetic  0.88 us (2%)
    pallas_call x1, Pallas kernels, body(): pl.pallas_call(functools.partial(kernel, subs, slabs, slots, dofs), out_s...  38 us
    unnamed x4, local copies, waits for them, and re-layouts  3.69 us
    reshape x2, local copies, waits for them, and re-layouts, body(): x = coarse_basis.reshape(FX * FY, dofs, columns).transpose(0, 2, 1)  2.24 us
    reshape x1, local copies, waits for them, and re-layouts, body(): out = out[:, :, :dofs].transpose(0, 2, 1).reshape(FX, FY, dofs * columns)  1.82 us

profile of v1, /device:TPU:1, one launch (start us, length us, event | category | flops | bytes accessed | tf_op | source)
XLA Modules:
  0.0 50.2 jit_solution(7784196259776041870)
XLA Ops:
  1.3 0.1 add_select_fusion
  1.4 0.8 %select_reduce_fusion = s32[60,20]{0,1:T(8,128)S(1)} fusion(s32[20,6]{0,1:T(8,128)S(1)} %add_select_fusion, s32[20,6]{0,1:T(8,128)} %param.8), kind=kLoop, calls=%fused_computation.1 | loop fusion | flops 20400 | bytes 5760 | tf_op jit(solution)/shard_map/reduce_sum | solution.py:358
  2.2 0.8 %copy.17 = s32[20,6]{1,0:T(8,128)S(1)} copy(s32[20,6]{0,1:T(8,128)} %param.8) | data formatting | bytes 960 | tf_op args[2]
  3.0 0.1 reshape.71
  3.1 0.1 copy.18
  3.2 0.1 reshape.72
  3.3 0.7 %concatenate.3.meta_ref = s32[1340]{0:T(1024)S(1)} concatenate(s32[120]{0:T(128)S(1)} %reshape.71, s32[20]{0:T(128)} %param.9, s32[1200]{0:T(1024)S(1)} %reshape.72), dimensions={0} | concatenate | bytes 10720 | tf_op jit(solution)/shard_map/concatenate | solution.py:361
  4.0 1.8 %reshape.70 = bf16[32,125,32]{2,1,0:T(8,128)(2,1)S(1)} reshape(bf16[4,8,4000]{2,1,0:T(8,128)(2,1)} %param.6) | data formatting | bytes 512000 | tf_op jit(solution)/shard_map/reshape | solution.py:352
  5.8 0.4 copy.16
  6.3 0.1 pad.4.x_ref
  6.3 0.0 copy-start
  6.3 2.9 %copy.19.jac_hbm = bf16[4,750,750]{2,1,0:T(8,128)(2,1)S(1)} copy(bf16[4,750,750]{2,0,1:T(4,128)(2,1)} %param.7) | data formatting | bytes 9000000 | tf_op args[1]
  9.2 0.0 copy-done
  9.2 38.0 %shard_map.77 = (bf16[32,32,128]{2,1,0:T(8,128)(2,1)S(1)}, f32[8,128]{1,0:T(8,128)S(1)}) custom-call(bf16[32,32,128]{2,1,0:T(8,128)(2,1)S(1)} %pad.4.x_ref, bf16[4,750,750]{2,1,0:T(8,128)(2,1)S(1)} %copy.19.jac_hbm, s32[1340]{0:T(1024)S(1)} %concatenate.3.meta_ref, s32[1,32]{1,0:T(1,128)S(1)} %copy-done), custom_call_target="tpu_custom_call" | custom-call | flops 1440000000 | bytes 4500000 | tf_op jit(solution)/shard_map/pallas_call | solution.py:368
  47.3 0.6 %slice.7 = f32[4,32]{1,0:T(4,128)} slice(f32[8,128]{1,0:T(8,128)S(1)} %get-tuple-element.5), slice={[0:4], [0:32]} | slice | bytes 1024 | tf_op jit(solution)/shard_map/slice | solution.py:417
  47.9 0.5 %copy.20 = bf16[32,125,32]{2,1,0:T(8,128)(2,1)S(1)} copy(bf16[32,125,32]{1,2,0:T(8,128)(2,1)S(1)} %slice_bitcast_fusion) | data formatting | bytes 512000 | tf_op jit(solution)/shard_map/transpose | solution.py:416
  48.4 1.8 %reshape.73 = bf16[4,8,4000]{2,1,0:T(8,128)(2,1)} reshape(bf16[32,125,32]{2,1,0:T(8,128)(2,1)S(1)} %copy.20) | data formatting | bytes 512000 | tf_op jit(solution)/shard_map/reshape | solution.py:416
  (4 shorter events, 0.0 us)
Async XLA Ops:
  6.3 2.9 %copy-start = (s32[1,32]{1,0:T(1,128)S(1)}, s32[1,32]{1,0:T(1,128)}, u32[]{:S(2)}) copy-start(s32[1,32]{1,0:T(1,128)} %ids_ref.1) | copy-start | bytes 388

commit v2 on v1

--- a/solution.py
+++ b/solution.py
@@ -14,21 +14,67 @@
 EY = FY + 2
 CELLS = EX * EY
 CV = 4
+TYPES = 4
 LANES = 128
 GROUP = 4
+GATHER = 4
 MESH = pl.DeviceIdType.MESH
 NT = (((1,), (1,)), ((), ()))
 
 
 def cell(r, c):
     return r * EY + c
+
+
+def group_count(slots):
+    return (slots + TYPES * (GROUP - 1)) // GROUP
+
+
+def index_lists(faces, kinds, count):
+    slots, groups = faces.shape[0], group_count(faces.shape[0])
+    i32 = jnp.int32
+    slot = jnp.arange(slots, dtype=i32)
+    live = slot < count
+    kind = jnp.where(live, kinds, TYPES)
+    earlier = slot[None, :] < slot[:, None]
+    same = kind[None, :] == kind[:, None]
+    place_in_kind = jnp.sum(jnp.where(same & earlier, 1, 0), axis=1)
+    place = place_in_kind + jnp.sum(jnp.where(kind[None, :] < kind[:, None], 1, 0), axis=1)
+    types = jnp.arange(TYPES, dtype=i32)
+    number = jnp.sum(jnp.where(kind[None, :] == types[:, None], 1, 0), axis=1)
+    needed = (number + GROUP - 1) // GROUP
+    before = types[None, :] < types[:, None]
+    first_group = jnp.sum(jnp.where(before, needed[None, :], 0), axis=1)
+    first_place = jnp.sum(jnp.where(before, number[None, :], 0), axis=1)
+    group = jnp.arange(groups, dtype=i32)
+    inside = (group[:, None] >= first_group[None, :]) & (
+        group[:, None] < (first_group + needed)[None, :]
+    )
+    group_type = jnp.sum(jnp.where(inside, types[None, :], 0), axis=1)
+    group_start = jnp.sum(
+        jnp.where(inside, first_place[None, :] + GROUP * (group[:, None] - first_group[None, :]), 0),
+        axis=1,
+    )
+    offset = jnp.sum(
+        jnp.where(kind[:, None] == types[None, :], GROUP * first_group[None, :], 0), axis=1
+    )
+    number_of_piece = (offset + place_in_kind)[:, None] * 6 + jnp.arange(1, 7, dtype=i32)[None, :]
+    number_of_piece = jnp.where(live[:, None], number_of_piece, 0)
+    cells = jnp.arange(CELLS, dtype=i32)
+    inverse = jnp.sum(
+        jnp.where(faces[None] == cells[:, None, None], number_of_piece[None], 0), axis=2
+    )
+    ordered = jnp.sum(
+        jnp.where((place[None, :] == slot[:, None])[:, :, None], faces[None], 0), axis=1
+    )
+    return jnp.concatenate([ordered.reshape(-1), group_type, group_start, inverse.reshape(-1)])
 
 
 def kernel(
     subs, slabs, slots, dofs,
     x_ref, jac_hbm, meta_ref, ids_ref,
     out_ref, coarse_ref,
-    field, jac, pieces, totals, sent, sent_cols, sent_diag, sent_cols_2,
+    field, jac, stacked, pieces, totals, sent, sent_cols, sent_diag, sent_cols_2,
     rim_cols, got_rows, got_cols, got_diag, got_rows_2, got_cols_2,
     dense, got_dense, row_sum, got_sum,
     jac_sem, s0, r0, s1, r1, s2, r2, cs1, cr1, cs2, cr2,
@@ -73,6 +119,8 @@
     def _(k):
         pieces[k] = jnp.zeros(pieces.shape[1:], f32)
 
+    for k in range(GROUP):
+        stacked[slots + k] = jnp.zeros(stacked.shape[1:], bf16)
     blank = jnp.zeros((columns, LANES), bf16)
     for c in (cell(0, 0), cell(0, EY - 1), cell(EX - 1, 0), cell(EX - 1, EY - 1)):
         field[c] = blank
@@ -146,23 +194,38 @@
         field[cell(r + 1, 0)] = rim_cols[0, r]
         field[cell(r + 1, EY - 1)] = rim_cols[1, r]
 
+    rows_in = columns * GROUP
+    groups = group_count(slots)
+    at_type = slots * 6
+    at_start = at_type + groups
+    at_inverse = at_start + groups
+
     def apply():
-        @pl.loop(0, slots // GROUP)
+        @pl.loop(0, slots // GATHER)
         def _(g):
-            for k in range(GROUP):
-                e = g * GROUP + k
+            for k in range(GATHER):
+                e = g * GATHER + k
                 x = jnp.concatenate(
                     [field[meta_ref[e * 6 + p]][:, :dofs] for p in range(6)], axis=1
                 )
-                y = lax.dot_general(
-                    x, jac[meta_ref[slots * 6 + e]], NT, preferred_element_type=f32
-                )
+                stacked[e] = x
+
+        @pl.loop(0, groups)
+        def _(g):
+            start = meta_ref[at_start + g]
+            x = stacked[pl.ds(start, GROUP)].reshape(rows_in, 6 * dofs)
+            y = lax.dot_general(
+                x, jac[meta_ref[at_type + g]], NT, preferred_element_type=f32
+            )
+            for k in range(GROUP):
                 for p in range(6):
-                    pieces[1 + e * 6 + p, :, :dofs] = y[:, p * dofs : (p + 1) * dofs]
+                    pieces[1 + (g * GROUP + k) * 6 + p, :, :dofs] = y[
+                        k * columns : (k + 1) * columns, p * dofs : (p + 1) * dofs
+                    ]
 
         @pl.loop(0, CELLS)
         def _(c):
-            base = slots * 7 + c * slots
+            base = at_inverse + c * slots
             total = pieces[meta_ref[base]]
             for e in range(1, slots):
                 total = total + pieces[meta_ref[base + e]]
@@ -239,12 +302,12 @@
         keep(left, cell(r, 0), v)
         keep(right, cell(r, EY - 1), w)
 
-    local = jnp.zeros((columns, columns), f32)
-    for r in range(FX):
-        for c in range(FY):
-            local = local + lax.dot_general(
-                x_ref[r * FY + c], field[cell(r + 1, c + 1)], NT, preferred_element_type=f32
-            )
+    own = range(FX * FY)
+    local = lax.dot_general(
+        jnp.concatenate([x_ref[k] for k in own], axis=1),
+        jnp.concatenate([field[cell(k // FY + 1, k % FY + 1)] for k in own], axis=1),
+        NT, preferred_element_type=f32,
+    )
     local = local * (1.0 / math.sqrt(FX * FY * dofs))
     ids = ids_ref[...]
     width = dense.shape[1]
@@ -351,14 +414,8 @@
 
     x = coarse_basis.reshape(FX * FY, dofs, columns).transpose(0, 2, 1)
     x = jnp.pad(x, ((0, 0), (0, 0), (0, LANES - dofs)))
-    slot = jnp.arange(slots, dtype=jnp.int32)
-    which = slot[:, None] * 6 + jnp.arange(1, 7, dtype=jnp.int32)[None, :]
-    which = jnp.where((slot < element_count[0])[:, None], which, 0)
-    cells = jnp.arange(CELLS, dtype=jnp.int32)
-    inverse = jnp.sum(
-        jnp.where(element_faces[None] == cells[:, None, None], which[None], 0), axis=2
-    )
-    meta = jnp.concatenate([element_faces.reshape(-1), element_type, inverse.reshape(-1)])
+    groups = group_count(slots)
+    meta = index_lists(element_faces, element_type, element_count[0])
 
     def block(*lead):
         return pltpu.VMEM((*lead, columns, LANES), bf16)
@@ -381,7 +438,8 @@
         scratch_shapes=[
             block(CELLS),
             pltpu.VMEM(jacobians.shape, bf16),
-            pltpu.VMEM((1 + 6 * slots, columns, LANES), f32),
+            pltpu.VMEM((slots + GROUP, columns, 6 * dofs), bf16),
+            pltpu.VMEM((1 + 6 * GROUP * groups, columns, LANES), f32),
             pltpu.VMEM((CELLS, columns, LANES), f32),
             block(CELLS),
             block(2, FX, 2),

time: 50.5 us -> 48 us (0.950)
  Pallas kernels: 38 us -> 34.7 us
  other arithmetic: 0.88 us -> 3.05 us
  local copies, waits for them, and re-layouts: 9.94 us -> 8.61 us
    pallas_call x1, Pallas kernels: 38 us -> 34.7 us  [body(): pl.pallas_call(functools.partial(kernel, subs, slabs, slots, dofs), out_s...]
    reduce_sum x1 -> x7, other arithmetic: 0.79 us -> 2.27 us  [the longest x1 0.86 us: index_lists(): jnp.sum(jnp.where((place[None, :] == slot[:, None])[:, :, None], faces[No...]
    unnamed x4 -> x3, local copies, waits for them, and re-layouts: 3.69 us -> 2.91 us
    select_n x1 -> x3, other arithmetic: 0.07 us -> 0.74 us  [the longest x1 0.66 us: index_lists(): kind = jnp.where(live, kinds, TYPES)]
    concatenate x1, local copies, waits for them, and re-layouts: 0.74 us -> 0.08 us  [index_lists(): jnp.concatenate([ordered.reshape(-1), group_type, group_start, inverse.re...]
where the time goes in v2:
time: 48 us; the launch traced here: 47.7 us
  Pallas kernels  34.7 us (72%)
  local copies, waits for them, and re-layouts  8.61 us (18%)
  other arithmetic  3.05 us (6%)
  between operations  1.38 us (3%)
    pallas_call x1, Pallas kernels, body(): pl.pallas_call(functools.partial(kernel, subs, slabs, slots, dofs), out_s...  34.7 us
    unnamed x3, local copies, waits for them, and re-layouts  2.91 us
    reshape x2, local copies, waits for them, and re-layouts, body(): x = coarse_basis.reshape(FX * FY, dofs, columns).transpose(0, 2, 1)  2.24 us
    reshape x1, local copies, waits for them, and re-layouts, body(): out = out[:, :, :dofs].transpose(0, 2, 1).reshape(FX, FY, dofs * columns)  1.82 us

profile of v2, /device:TPU:1, one launch (start us, length us, event | category | flops | bytes accessed | tf_op | source)
XLA Modules:
  0.0 47.7 jit_solution(9449828749410263096)
XLA Ops:
  1.3 0.7 %broadcast_select_fusion = s32[20]{0:T(128)S(1)} fusion(s32[20]{0:T(128)} %param.9, s32[]{:T(128)} %bitcast.5), kind=kLoop, calls=%fused_computation.30 | loop fusion | flops 40 | bytes 164 | tf_op jit(solution)/shard_map/jit(_where)/select_n | solution.py:38
  1.9 0.1 select_reduce_fusion.9
  2.1 0.1 select_reduce_fusion.6
  2.3 0.1 select_reduce_fusion.4
  2.3 0.1 select_reduce_fusion.5
  2.4 0.2 select_reduce_fusion.2
  2.6 0.1 add_select_fusion
  2.7 0.9 %select_reduce_fusion.1 = s32[20,6]{0,1:T(8,128)S(1)} fusion(s32[20,6]{0,1:T(8,128)} %param.8, pred[20,20]{1,0:T(8,128)(4,1)S(1)} %iota_compare_fusion.1), kind=kLoop, calls=%fused_computation.3 | loop fusion | flops 4680 | bytes 1360 | tf_op jit(solution)/shard_map/reduce_sum | solution.py:67
  3.6 0.1 copy.17
  3.7 0.1 reshape.129
  3.8 0.8 %select_reduce_fusion = s32[60,20]{0,1:T(8,128)S(1)} fusion(s32[20,6]{0,1:T(8,128)S(1)} %add_select_fusion, s32[20,6]{0,1:T(8,128)} %param.8), kind=kLoop, calls=%fused_computation.1 | loop fusion | flops 20400 | bytes 5760 | tf_op jit(solution)/shard_map/reduce_sum | solution.py:64
  4.6 0.1 copy.18
  4.7 0.1 reshape.130
  4.8 0.1 concatenate.3.meta_ref
  4.9 1.8 %reshape.128 = bf16[32,125,32]{2,1,0:T(8,128)(2,1)S(1)} reshape(bf16[4,8,4000]{2,1,0:T(8,128)(2,1)} %param.6) | data formatting | bytes 512000 | tf_op jit(solution)/shard_map/reshape | solution.py:415
  6.7 0.4 copy.16
  7.1 0.1 pad.4.x_ref
  7.2 0.0 copy-start
  7.2 2.9 %copy.19.jac_hbm = bf16[4,750,750]{2,1,0:T(8,128)(2,1)S(1)} copy(bf16[4,750,750]{2,0,1:T(4,128)(2,1)} %param.7) | data formatting | bytes 9000000 | tf_op args[1]
  10.1 0.0 copy-done
  10.1 34.7 %shard_map.77 = (bf16[32,32,128]{2,1,0:T(8,128)(2,1)S(1)}, f32[8,128]{1,0:T(8,128)S(1)}) custom-call(bf16[32,32,128]{2,1,0:T(8,128)(2,1)S(1)} %pad.4.x_ref, bf16[4,750,750]{2,1,0:T(8,128)(2,1)S(1)} %copy.19.jac_hbm, s32[1336]{0:T(1024)S(1)} %concatenate.3.meta_ref, s32[1,32]{1,0:T(1,128)S(1)} %copy-done), custom_call_target="tpu_custom_call" | custom-call | flops 1440000000 | bytes 4500000 | tf_op jit(solution)/shard_map/pallas_call | solution.py:425
  44.8 0.6 %slice.7 = f32[4,32]{1,0:T(4,128)} slice(f32[8,128]{1,0:T(8,128)S(1)} %get-tuple-element.5), slice={[0:4], [0:32]} | slice | bytes 1024 | tf_op jit(solution)/shard_map/slice | solution.py:475
  45.4 0.5 %copy.20 = bf16[32,125,32]{2,1,0:T(8,128)(2,1)S(1)} copy(bf16[32,125,32]{1,2,0:T(8,128)(2,1)S(1)} %slice_bitcast_fusion) | data formatting | bytes 512000 | tf_op jit(solution)/shard_map/transpose | solution.py:474
  45.9 1.8 %reshape.131 = bf16[4,8,4000]{2,1,0:T(8,128)(2,1)} reshape(bf16[32,125,32]{2,1,0:T(8,128)(2,1)S(1)} %copy.20) | data formatting | bytes 512000 | tf_op jit(solution)/shard_map/reshape | solution.py:474
  (7 shorter events, 0.1 us)
Async XLA Ops:
  7.2 2.9 %copy-start = (s32[1,32]{1,0:T(1,128)S(1)}, s32[1,32]{1,0:T(1,128)}, u32[]{:S(2)}) copy-start(s32[1,32]{1,0:T(1,128)} %ids_ref.1) | copy-start | bytes 388

commit v3 on v2

--- a/solution.py
+++ b/solution.py
@@ -18,6 +18,8 @@
 LANES = 128
 GROUP = 4
 GATHER = 4
+SUMS = 8
+SPREAD = 4
 MESH = pl.DeviceIdType.MESH
 NT = (((1,), (1,)), ((), ()))
 
@@ -30,54 +32,74 @@
     return (slots + TYPES * (GROUP - 1)) // GROUP
 
 
-def index_lists(faces, kinds, count):
-    slots, groups = faces.shape[0], group_count(faces.shape[0])
+def index_lists(faces_ref, kinds_ref, count, lists):
+    slots, groups = faces_ref.shape[1], group_count(faces_ref.shape[1])
     i32 = jnp.int32
-    slot = jnp.arange(slots, dtype=i32)
-    live = slot < count
-    kind = jnp.where(live, kinds, TYPES)
-    earlier = slot[None, :] < slot[:, None]
-    same = kind[None, :] == kind[:, None]
-    place_in_kind = jnp.sum(jnp.where(same & earlier, 1, 0), axis=1)
-    place = place_in_kind + jnp.sum(jnp.where(kind[None, :] < kind[:, None], 1, 0), axis=1)
-    types = jnp.arange(TYPES, dtype=i32)
-    number = jnp.sum(jnp.where(kind[None, :] == types[:, None], 1, 0), axis=1)
-    needed = (number + GROUP - 1) // GROUP
-    before = types[None, :] < types[:, None]
-    first_group = jnp.sum(jnp.where(before, needed[None, :], 0), axis=1)
-    first_place = jnp.sum(jnp.where(before, number[None, :], 0), axis=1)
-    group = jnp.arange(groups, dtype=i32)
-    inside = (group[:, None] >= first_group[None, :]) & (
-        group[:, None] < (first_group + needed)[None, :]
-    )
-    group_type = jnp.sum(jnp.where(inside, types[None, :], 0), axis=1)
-    group_start = jnp.sum(
-        jnp.where(inside, first_place[None, :] + GROUP * (group[:, None] - first_group[None, :]), 0),
-        axis=1,
-    )
-    offset = jnp.sum(
-        jnp.where(kind[:, None] == types[None, :], GROUP * first_group[None, :], 0), axis=1
-    )
-    number_of_piece = (offset + place_in_kind)[:, None] * 6 + jnp.arange(1, 7, dtype=i32)[None, :]
-    number_of_piece = jnp.where(live[:, None], number_of_piece, 0)
-    cells = jnp.arange(CELLS, dtype=i32)
-    inverse = jnp.sum(
-        jnp.where(faces[None] == cells[:, None, None], number_of_piece[None], 0), axis=2
-    )
-    ordered = jnp.sum(
-        jnp.where((place[None, :] == slot[:, None])[:, :, None], faces[None], 0), axis=1
-    )
-    return jnp.concatenate([ordered.reshape(-1), group_type, group_start, inverse.reshape(-1)])
+
+    def iota(rows, cols, axis):
+        return lax.broadcasted_iota(i32, (rows, cols), axis)
+
+    def count_of(mask, axis):
+        return jnp.sum(jnp.where(mask, 1, 0), axis=axis, keepdims=True)
+
+    def as_column(row):
+        n = row.shape[1]
+        return jnp.sum(jnp.where(iota(n, n, 0) == iota(n, n, 1), row, 0), axis=1, keepdims=True)
+
+    def put(lane, column):
+        lists[pl.ds(0, column.shape[0]), lane : lane + 1] = column
+
+    lists[...] = jnp.zeros(lists.shape, i32)
+    live = iota(1, slots, 1) < count
+    kind = jnp.where(live, kinds_ref[...], TYPES)
+    kind_col = as_column(kind)
+    earlier = iota(slots, slots, 0) < iota(slots, slots, 1)
+    in_kind = count_of((kind_col == kind) & earlier, 0)
+    place = in_kind + count_of(kind_col < kind, 0)
+    group = iota(groups, 1, 0)
+    group_type = jnp.zeros((groups, 1), i32)
+    group_start = jnp.zeros((groups, 1), i32)
+    position = in_kind
+    first_group = jnp.zeros((1, 1), i32)
+    first_place = jnp.zeros((1, 1), i32)
+    for t in range(TYPES):
+        number = count_of(kind == t, 1)
+        needed = lax.shift_right_logical(number + (GROUP - 1), 2)
+        inside = (group >= first_group) & (group < first_group + needed)
+        group_type = jnp.where(inside, t, group_type)
+        group_start = jnp.where(inside, first_place + GROUP * (group - first_group), group_start)
+        position = position + jnp.where(kind == t, GROUP * first_group, 0)
+        first_group = first_group + needed
+        first_place = first_place + number
+    faces = [faces_ref[p : p + 1, :] for p in range(6)]
+    cells = jnp.concatenate([jnp.where(live, f, CELLS) for f in faces], axis=1)
+    piece = jnp.concatenate([position * 6 + p for p in range(6)], axis=1)
+    total = 6 * slots
+    cells_col = as_column(cells)
+    before = iota(total, total, 0) < iota(total, total, 1)
+    in_cell = count_of((cells_col == cells) & before, 0)
+    rank = in_cell + count_of(cells_col < cells, 0)
+    chosen = rank == iota(total, 1, 0)
+    put(0, jnp.sum(jnp.where(chosen, piece, 0), axis=1, keepdims=True))
+    put(1, jnp.sum(jnp.where(chosen, jnp.where(in_cell == 0, 1, 0), 0), axis=1, keepdims=True))
+    spot = iota(CELLS, 1, 0)
+    upto = count_of(cells <= spot, 1)
+    put(2, jnp.where(count_of(cells == spot, 1) > 0, upto, 0))
+    taken = place == iota(slots, 1, 0)
+    for p in range(6):
+        put(3 + p, jnp.sum(jnp.where(taken, faces[p], 0), axis=1, keepdims=True))
+    put(9, group_type)
+    put(10, group_start)
 
 
 def kernel(
     subs, slabs, slots, dofs,
-    x_ref, jac_hbm, meta_ref, ids_ref,
+    x_ref, jac, faces_ref, kinds_ref, count_ref, ids_ref,
     out_ref, coarse_ref,
-    field, jac, stacked, pieces, totals, sent, sent_cols, sent_diag, sent_cols_2,
+    field, lists, meta_ref, stacked, pieces, running, totals, sent, sent_cols, sent_diag, sent_cols_2,
     rim_cols, got_rows, got_cols, got_diag, got_rows_2, got_cols_2,
     dense, got_dense, row_sum, got_sum,
-    jac_sem, s0, r0, s1, r1, s2, r2, cs1, cr1, cs2, cr2,
+    list_sem, s0, r0, s1, r1, s2, r2, cs1, cr1, cs2, cr2,
 ):
     i = lax.axis_index("sub")
     j = lax.axis_index("slab")
@@ -86,9 +108,6 @@
     f32 = jnp.float32
     bf16 = jnp.bfloat16
 
-    jac_copy = pltpu.make_async_copy(jac_hbm, jac, jac_sem)
-    jac_copy.start()
-
     barrier = pltpu.get_barrier_semaphore()
 
     def greet(di, dj):
@@ -115,10 +134,15 @@
         def _():
             greet(di, dj)
 
+    index_lists(faces_ref, kinds_ref, count_ref[0], lists)
+    list_copy = pltpu.make_async_copy(lists, meta_ref, list_sem)
+    list_copy.start()
+
     @pl.loop(0, pieces.shape[0])
     def _(k):
         pieces[k] = jnp.zeros(pieces.shape[1:], f32)
 
+    running[0] = jnp.zeros(running.shape[1:], f32)
     for k in range(GROUP):
         stacked[slots + k] = jnp.zeros(stacked.shape[1:], bf16)
     blank = jnp.zeros((columns, LANES), bf16)
@@ -188,7 +212,7 @@
         (right, left, remote(x_cols.at[:, FY - 1], rim_cols.at[0], s0.at[3], r0.at[3], i, j + 1)),
     )
     exchange(first)
-    jac_copy.wait()
+    list_copy.wait()
     arrive(first)
     for r in range(FX):
         field[cell(r + 1, 0)] = rim_cols[0, r]
@@ -196,9 +220,6 @@
 
     rows_in = columns * GROUP
     groups = group_count(slots)
-    at_type = slots * 6
-    at_start = at_type + groups
-    at_inverse = at_start + groups
 
     def apply():
         @pl.loop(0, slots // GATHER)
@@ -206,31 +227,39 @@
             for k in range(GATHER):
                 e = g * GATHER + k
                 x = jnp.concatenate(
-                    [field[meta_ref[e * 6 + p]][:, :dofs] for p in range(6)], axis=1
+                    [field[meta_ref[e, 3 + p]][:, :dofs] for p in range(6)], axis=1
                 )
                 stacked[e] = x
 
         @pl.loop(0, groups)
         def _(g):
-            start = meta_ref[at_start + g]
+            start = meta_ref[g, 10]
             x = stacked[pl.ds(start, GROUP)].reshape(rows_in, 6 * dofs)
             y = lax.dot_general(
-                x, jac[meta_ref[at_type + g]], NT, preferred_element_type=f32
+                x, jac[meta_ref[g, 9]], NT, preferred_element_type=f32
             )
             for k in range(GROUP):
                 for p in range(6):
-                    pieces[1 + (g * GROUP + k) * 6 + p, :, :dofs] = y[
+                    pieces[(g * GROUP + k) * 6 + p, :, :dofs] = y[
                         k * columns : (k + 1) * columns, p * dofs : (p + 1) * dofs
                     ]
 
-        @pl.loop(0, CELLS)
-        def _(c):
-            base = at_inverse + c * slots
-            total = pieces[meta_ref[base]]
-            for e in range(1, slots):
-                total = total + pieces[meta_ref[base + e]]
-            totals[c] = total
-            sent[c] = total.astype(bf16)
+        def add(n, total):
+            for k in range(SUMS):
+                at = n * SUMS + k
+                total = jnp.where(meta_ref[at, 1] > 0, 0.0, total) + pieces[meta_ref[at, 0]]
+                running[1 + at] = total
+            return total
+
+        lax.fori_loop(0, 6 * slots // SUMS, add, jnp.zeros((columns, LANES), f32))
+
+        @pl.loop(0, CELLS // SPREAD)
+        def _(n):
+            for k in range(SPREAD):
+                c = n * SPREAD + k
+                total = running[meta_ref[c, 2]]
+                totals[c] = total
+                sent[c] = total.astype(bf16)
 
     apply()
     for r in range(FX):
@@ -415,7 +444,6 @@
     x = coarse_basis.reshape(FX * FY, dofs, columns).transpose(0, 2, 1)
     x = jnp.pad(x, ((0, 0), (0, 0), (0, LANES - dofs)))
     groups = group_count(slots)
-    meta = index_lists(element_faces, element_type, element_count[0])
 
     def block(*lead):
         return pltpu.VMEM((*lead, columns, LANES), bf16)
@@ -430,16 +458,20 @@
         ),
         in_specs=[
             vmem,
-            pl.BlockSpec(memory_space=pl.ANY),
+            vmem,
+            vmem,
+            vmem,
             pl.BlockSpec(memory_space=pltpu.SMEM),
             vmem,
         ],
         out_specs=(vmem, vmem),
         scratch_shapes=[
             block(CELLS),
-            pltpu.VMEM(jacobians.shape, bf16),
+            pltpu.VMEM((6 * slots, LANES), jnp.int32),
+            pltpu.SMEM((6 * slots, LANES), jnp.int32),
             pltpu.VMEM((slots + GROUP, columns, 6 * dofs), bf16),
-            pltpu.VMEM((1 + 6 * GROUP * groups, columns, LANES), f32),
+            pltpu.VMEM((6 * GROUP * groups, columns, LANES), f32),
+            pltpu.VMEM((1 + 6 * slots, columns, LANES), f32),
             pltpu.VMEM((CELLS, columns, LANES), f32),
             block(CELLS),
             block(2, FX, 2),
@@ -470,7 +502,7 @@
             bytes_accessed=2 * jacobians.size,
             transcendentals=0,
         ),
-    )(x, jacobians, meta, vertex_ids)
+    )(x, jacobians, element_faces.T, element_type.reshape(1, slots), element_count, vertex_ids)
     out = out[:, :, :dofs].transpose(0, 2, 1).reshape(FX, FY, dofs * columns)
     return out, coarse[:CV, :vertex_total]
 

time: 48 us -> 40.7 us (0.85)
  Pallas kernels: 34.7 us -> 31 us
  other arithmetic: 3.05 us -> 0 us
    pallas_call x1, Pallas kernels: 34.7 us -> 31 us  [body(): pl.pallas_call(functools.partial(kernel, subs, slabs, slots, dofs), out_s...]
    reduce_sum x7 -> x0, other arithmetic: 2.27 us -> none  [the longest x1 0.86 us: index_lists(): jnp.sum(jnp.where((place[None, :] == slot[:, None])[:, :, None], faces[No...]
    select_n x3 -> x0, other arithmetic: 0.74 us -> none  [the longest x1 0.66 us: index_lists(): kind = jnp.where(live, kinds, TYPES)]
    unnamed x3 -> x7, local copies, waits for them, and re-layouts: 2.91 us -> 2.93 us
where the time goes in v3:
time: 40.7 us; the launch traced here: 40.5 us
  Pallas kernels  31 us (76%)
  local copies, waits for them, and re-layouts  8.14 us (20%)
  between operations  1.37 us (3%)
    pallas_call x1, Pallas kernels, body(): pl.pallas_call(functools.partial(kernel, subs, slabs, slots, dofs), out_s...  31 us
    unnamed x7, local copies, waits for them, and re-layouts  2.93 us
    reshape x2, local copies, waits for them, and re-layouts, body(): x = coarse_basis.reshape(FX * FY, dofs, columns).transpose(0, 2, 1)  2.23 us
    reshape x1, local copies, waits for them, and re-layouts, body(): out = out[:, :, :dofs].transpose(0, 2, 1).reshape(FX, FY, dofs * columns)  1.82 us

profile of v3, /device:TPU:1, one launch (start us, length us, event | category | flops | bytes accessed | tf_op | source)
XLA Modules:
  0.0 40.5 jit_solution(17801987286155847730)
XLA Ops:
  1.3 1.8 %reshape.13 = bf16[32,125,32]{2,1,0:T(8,128)(2,1)S(1)} reshape(bf16[4,8,4000]{2,1,0:T(8,128)(2,1)} %param.6) | data formatting | bytes 512000 | tf_op jit(solution)/shard_map/reshape | solution.py:444
  3.1 0.4 %copy.9 = bf16[32,125,32]{1,2,0:T(8,128)(2,1)S(1)} copy(bf16[32,125,32]{2,1,0:T(8,128)(2,1)S(1)} %reshape.13) | data formatting | bytes 512000 | tf_op jit(solution)/shard_map/reshape | solution.py:444
  3.5 0.1 pad.4.x_ref
  3.6 0.0 copy-start
  3.6 0.0 copy-start.1
  3.6 0.0 copy-start.2
  3.6 2.9 %copy.10.jac = bf16[4,750,750]{2,1,0:T(8,128)(2,1)S(1)} copy(bf16[4,750,750]{2,0,1:T(4,128)(2,1)} %param.7) | data formatting | bytes 9000000 | tf_op args[1]
  6.5 0.0 copy-done
  6.5 0.0 copy-done.1
  6.6 0.0 copy-done.2
  6.6 31.0 %shard_map.77 = (bf16[32,32,128]{2,1,0:T(8,128)(2,1)S(1)}, f32[8,128]{1,0:T(8,128)S(1)}) custom-call(bf16[32,32,128]{2,1,0:T(8,128)(2,1)S(1)} %pad.4.x_ref, bf16[4,750,750]{2,1,0:T(8,128)(2,1)S(1)} %copy.10.jac, s32[6,20]{1,0:T(8,128)S(1)} %bitcast.5, s32[1,20]{1,0:T(1,128)S(1)} %bitcast.6, s32[1]{0:T(128)S(6)} %copy.12.count_ref, s32[1,32]{1,0:T(1,128)S(1)} %copy-done.2), custom_call_target="tpu_custom_call" | custom-call | flops 1440000000 | bytes 4500000 | tf_op jit(solution)/shard_map/pallas_call | solution.py:453
  37.6 0.6 %slice.7 = f32[4,32]{1,0:T(4,128)} slice(f32[8,128]{1,0:T(8,128)S(1)} %get-tuple-element.5), slice={[0:4], [0:32]} | slice | bytes 1024 | tf_op jit(solution)/shard_map/slice | solution.py:507
  38.2 0.5 %copy.11 = bf16[32,125,32]{2,1,0:T(8,128)(2,1)S(1)} copy(bf16[32,125,32]{1,2,0:T(8,128)(2,1)S(1)} %slice_bitcast_fusion) | data formatting | bytes 512000 | tf_op jit(solution)/shard_map/transpose | solution.py:506
  38.7 1.8 %reshape.15 = bf16[4,8,4000]{2,1,0:T(8,128)(2,1)} reshape(bf16[32,125,32]{2,1,0:T(8,128)(2,1)S(1)} %copy.11) | data formatting | bytes 512000 | tf_op jit(solution)/shard_map/reshape | solution.py:506
  (1 shorter events, 0.0 us)
Async XLA Ops:
  3.6 2.9 %copy-start = (s32[20,6]{0,1:T(8,128)S(1)}, s32[20,6]{0,1:T(8,128)}, u32[]{:S(2)}) copy-start(s32[20,6]{0,1:T(8,128)} %param.8) | copy-start | bytes 1444
  3.6 2.9 %copy-start.1 = (s32[20]{0:T(128)S(1)}, s32[20]{0:T(128)}, u32[]{:S(2)}) copy-start(s32[20]{0:T(128)} %param.9) | copy-start | bytes 244
  3.6 2.9 %copy-start.2 = (s32[1,32]{1,0:T(1,128)S(1)}, s32[1,32]{1,0:T(1,128)}, u32[]{:S(2)}) copy-start(s32[1,32]{1,0:T(1,128)} %ids_ref.1) | copy-start | bytes 388

commit v4 on v3

--- a/solution.py
+++ b/solution.py
@@ -18,6 +18,7 @@
 LANES = 128
 GROUP = 4
 GATHER = 4
+TOGETHER = 2
 SUMS = 8
 SPREAD = 4
 MESH = pl.DeviceIdType.MESH
@@ -94,9 +95,9 @@
 
 def kernel(
     subs, slabs, slots, dofs,
-    x_ref, jac, faces_ref, kinds_ref, count_ref, ids_ref,
+    x_ref, jac_ref, faces_ref, kinds_ref, count_ref, ids_ref,
     out_ref, coarse_ref,
-    field, lists, meta_ref, stacked, pieces, running, totals, sent, sent_cols, sent_diag, sent_cols_2,
+    field, lists, meta_ref, jac, stacked, pieces, running, totals, sent, sent_cols, sent_diag, sent_cols_2,
     rim_cols, got_rows, got_cols, got_diag, got_rows_2, got_cols_2,
     dense, got_dense, row_sum, got_sum,
     list_sem, s0, r0, s1, r1, s2, r2, cs1, cr1, cs2, cr2,
@@ -137,10 +138,6 @@
     index_lists(faces_ref, kinds_ref, count_ref[0], lists)
     list_copy = pltpu.make_async_copy(lists, meta_ref, list_sem)
     list_copy.start()
-
-    @pl.loop(0, pieces.shape[0])
-    def _(k):
-        pieces[k] = jnp.zeros(pieces.shape[1:], f32)
 
     running[0] = jnp.zeros(running.shape[1:], f32)
     for k in range(GROUP):
@@ -212,6 +209,20 @@
         (right, left, remote(x_cols.at[:, FY - 1], rim_cols.at[0], s0.at[3], r0.at[3], i, j + 1)),
     )
     exchange(first)
+
+    @pl.loop(0, TYPES * 6)
+    def _(n):
+        t, r = n // 6, n % 6
+        top = pl.multiple_of(r * LANES, LANES)
+        face_rows = jac_ref[t, r]
+        end = jnp.zeros((dofs, LANES - dofs), bf16)
+        for p in range(6):
+            lanes = slice(p * LANES, (p + 1) * LANES)
+            jac[t, pl.ds(top + LANES - 16, 16), lanes] = jnp.zeros((16, LANES), bf16)
+            jac[t, pl.ds(top, dofs), lanes] = jnp.concatenate(
+                [face_rows[:, p * dofs : (p + 1) * dofs], end], axis=1
+            )
+
     list_copy.wait()
     arrive(first)
     for r in range(FX):
@@ -226,23 +237,20 @@
         def _(g):
             for k in range(GATHER):
                 e = g * GATHER + k
-                x = jnp.concatenate(
-                    [field[meta_ref[e, 3 + p]][:, :dofs] for p in range(6)], axis=1
-                )
-                stacked[e] = x
-
-        @pl.loop(0, groups)
-        def _(g):
-            start = meta_ref[g, 10]
-            x = stacked[pl.ds(start, GROUP)].reshape(rows_in, 6 * dofs)
-            y = lax.dot_general(
-                x, jac[meta_ref[g, 9]], NT, preferred_element_type=f32
-            )
-            for k in range(GROUP):
                 for p in range(6):
-                    pieces[(g * GROUP + k) * 6 + p, :, :dofs] = y[
-                        k * columns : (k + 1) * columns, p * dofs : (p + 1) * dofs
-                    ]
+                    stacked[e, :, p * LANES : (p + 1) * LANES] = field[meta_ref[e, 3 + p]]
+
+        @pl.loop(0, groups // TOGETHER)
+        def _(n):
+            for m in range(TOGETHER):
+                g = n * TOGETHER + m
+                x = stacked[pl.ds(meta_ref[g, 10], GROUP)].reshape(rows_in, 6 * LANES)
+                y = lax.dot_general(x, jac[meta_ref[g, 9]], NT, preferred_element_type=f32)
+                for k in range(GROUP):
+                    for p in range(6):
+                        pieces[(g * GROUP + k) * 6 + p] = y[
+                            k * columns : (k + 1) * columns, p * LANES : (p + 1) * LANES
+                        ]
 
         def add(n, total):
             for k in range(SUMS):
@@ -444,6 +452,7 @@
     x = coarse_basis.reshape(FX * FY, dofs, columns).transpose(0, 2, 1)
     x = jnp.pad(x, ((0, 0), (0, 0), (0, LANES - dofs)))
     groups = group_count(slots)
+    jac = jacobians.reshape(TYPES, 6, dofs, 6 * dofs)
 
     def block(*lead):
         return pltpu.VMEM((*lead, columns, LANES), bf16)
@@ -469,7 +478,8 @@
             block(CELLS),
             pltpu.VMEM((6 * slots, LANES), jnp.int32),
             pltpu.SMEM((6 * slots, LANES), jnp.int32),
-            pltpu.VMEM((slots + GROUP, columns, 6 * dofs), bf16),
+            pltpu.VMEM((TYPES, 6 * LANES, 6 * LANES), bf16),
+            pltpu.VMEM((slots + GROUP, columns, 6 * LANES), bf16),
             pltpu.VMEM((6 * GROUP * groups, columns, LANES), f32),
             pltpu.VMEM((1 + 6 * slots, columns, LANES), f32),
             pltpu.VMEM((CELLS, columns, LANES), f32),
@@ -502,7 +512,7 @@
             bytes_accessed=2 * jacobians.size,
             transcendentals=0,
         ),
-    )(x, jacobians, element_faces.T, element_type.reshape(1, slots), element_count, vertex_ids)
+    )(x, jac, element_faces.T, element_type.reshape(1, slots), element_count, vertex_ids)
     out = out[:, :, :dofs].transpose(0, 2, 1).reshape(FX, FY, dofs * columns)
     return out, coarse[:CV, :vertex_total]
 

time: 40.7 us -> 37.5 us (0.921)
  Pallas kernels: 31 us -> 27.4 us
    pallas_call x1, Pallas kernels: 31 us -> 27.4 us  [body(): pl.pallas_call(functools.partial(kernel, subs, slabs, slots, dofs), out_s...]
    reshape x0 -> x1, local copies, waits for them, and re-layouts: none -> 3.1 us  [body(): jac = jacobians.reshape(TYPES, 6, dofs, 6 * dofs)]
    unnamed x7 -> x6, local copies, waits for them, and re-layouts: 2.93 us -> 0.02 us
where the time goes in v4:
time: 37.5 us; the launch traced here: 37.1 us
  Pallas kernels  27.4 us (73%)
  local copies, waits for them, and re-layouts  8.33 us (22%)
  between operations  1.37 us (4%)
    pallas_call x1, Pallas kernels, body(): pl.pallas_call(functools.partial(kernel, subs, slabs, slots, dofs), out_s...  27.4 us
    reshape x1, local copies, waits for them, and re-layouts, body(): jac = jacobians.reshape(TYPES, 6, dofs, 6 * dofs)  3.1 us
    reshape x2, local copies, waits for them, and re-layouts, body(): x = coarse_basis.reshape(FX * FY, dofs, columns).transpose(0, 2, 1)  2.23 us
    reshape x1, local copies, waits for them, and re-layouts, body(): out = out[:, :, :dofs].transpose(0, 2, 1).reshape(FX, FY, dofs * columns)  1.82 us

profile of v4, /device:TPU:1, one launch (start us, length us, event | category | flops | bytes accessed | tf_op | source)
XLA Modules:
  0.0 37.1 jit_solution(16706976630503360695)
XLA Ops:
  1.3 1.8 %reshape.16 = bf16[32,125,32]{2,1,0:T(8,128)(2,1)S(1)} reshape(bf16[4,8,4000]{2,1,0:T(8,128)(2,1)} %param.6) | data formatting | bytes 512000 | tf_op jit(solution)/shard_map/reshape | solution.py:452
  3.1 0.4 %copy.9 = bf16[32,125,32]{1,2,0:T(8,128)(2,1)S(1)} copy(bf16[32,125,32]{2,1,0:T(8,128)(2,1)S(1)} %reshape.16) | data formatting | bytes 512000 | tf_op jit(solution)/shard_map/reshape | solution.py:452
  3.5 0.1 pad.4.x_ref
  3.6 0.0 copy-start
  3.6 0.0 copy-start.1
  3.6 0.0 copy-start.2
  3.6 3.1 %copy.12.jac_ref = bf16[4,6,125,750]{3,2,1,0:T(8,128)(2,1)S(1)} copy(bf16[4,6,125,750]{3,0,2,1:T(4,128)(2,1)} %bitcast.8) | data formatting | bytes 9000000 | tf_op jit(solution)/shard_map/reshape | solution.py:455
  6.7 0.0 copy-done
  6.7 0.0 copy-done.1
  6.8 0.0 copy-done.2
  6.8 27.4 %shard_map.77 = (bf16[32,32,128]{2,1,0:T(8,128)(2,1)S(1)}, f32[8,128]{1,0:T(8,128)S(1)}) custom-call(bf16[32,32,128]{2,1,0:T(8,128)(2,1)S(1)} %pad.4.x_ref, bf16[4,6,125,750]{3,2,1,0:T(8,128)(2,1)S(1)} %copy.12.jac_ref, s32[6,20]{1,0:T(8,128)S(1)} %bitcast.6, s32[1,20]{1,0:T(1,128)S(1)} %bitcast.7, s32[1]{0:T(128)S(6)} %copy.13.count_ref, s32[1,32]{1,0:T(1,128)S(1)} %copy-done.2), custom_call_target="tpu_custom_call" | custom-call | flops 1440000000 | bytes 4500000 | tf_op jit(solution)/shard_map/pallas_call | solution.py:462
  34.2 0.6 %slice.7 = f32[4,32]{1,0:T(4,128)} slice(f32[8,128]{1,0:T(8,128)S(1)} %get-tuple-element.5), slice={[0:4], [0:32]} | slice | bytes 1024 | tf_op jit(solution)/shard_map/slice | solution.py:517
  34.8 0.5 %copy.11 = bf16[32,125,32]{2,1,0:T(8,128)(2,1)S(1)} copy(bf16[32,125,32]{1,2,0:T(8,128)(2,1)S(1)} %slice_bitcast_fusion) | data formatting | bytes 512000 | tf_op jit(solution)/shard_map/transpose | solution.py:516
  35.3 1.8 %reshape.19 = bf16[4,8,4000]{2,1,0:T(8,128)(2,1)} reshape(bf16[32,125,32]{2,1,0:T(8,128)(2,1)S(1)} %copy.11) | data formatting | bytes 512000 | tf_op jit(solution)/shard_map/reshape | solution.py:516
  (1 shorter events, 0.0 us)
Async XLA Ops:
  3.6 3.2 %copy-start = (s32[20,6]{0,1:T(8,128)S(1)}, s32[20,6]{0,1:T(8,128)}, u32[]{:S(2)}) copy-start(s32[20,6]{0,1:T(8,128)} %param.8) | copy-start | bytes 1444
  3.6 3.1 %copy-start.1 = (s32[20]{0:T(128)S(1)}, s32[20]{0:T(128)}, u32[]{:S(2)}) copy-start(s32[20]{0:T(128)} %param.9) | copy-start | bytes 244
  3.6 3.1 %copy-start.2 = (s32[1,32]{1,0:T(1,128)S(1)}, s32[1,32]{1,0:T(1,128)}, u32[]{:S(2)}) copy-start(s32[1,32]{1,0:T(1,128)} %ids_ref.1) | copy-start | bytes 388

commit v5 on v4

--- a/solution.py
+++ b/solution.py
@@ -18,7 +18,7 @@
 LANES = 128
 GROUP = 4
 GATHER = 4
-TOGETHER = 2
+TOGETHER = 4
 SUMS = 8
 SPREAD = 4
 MESH = pl.DeviceIdType.MESH
@@ -93,13 +93,19 @@
     put(10, group_start)
 
 
+def two_parts(x, axis):
+    high = x.astype(jnp.bfloat16)
+    rest = (x - high.astype(jnp.float32)).astype(jnp.bfloat16)
+    return jnp.concatenate([high, rest], axis=axis)
+
+
 def kernel(
     subs, slabs, slots, dofs,
     x_ref, jac_ref, faces_ref, kinds_ref, count_ref, ids_ref,
     out_ref, coarse_ref,
     field, lists, meta_ref, jac, stacked, pieces, running, totals, sent, sent_cols, sent_diag, sent_cols_2,
     rim_cols, got_rows, got_cols, got_diag, got_rows_2, got_cols_2,
-    dense, got_dense, row_sum, got_sum,
+    one_hot, row_hot, dense, got_dense, row_sum, got_sum,
     list_sem, s0, r0, s1, r1, s2, r2, cs1, cr1, cs2, cr2,
 ):
     i = lax.axis_index("sub")
@@ -138,6 +144,13 @@
     index_lists(faces_ref, kinds_ref, count_ref[0], lists)
     list_copy = pltpu.make_async_copy(lists, meta_ref, list_sem)
     list_copy.start()
+
+    ids = jnp.concatenate([ids_ref[...]] * 2, axis=1)
+    spots = lax.broadcasted_iota(jnp.int32, one_hot.shape, 0)
+    one_hot[...] = jnp.where(spots == ids, 1.0, 0.0).astype(bf16)
+    rows = lax.broadcasted_iota(jnp.int32, row_hot.shape, 0)
+    spot = jnp.where(rows % 8 < CV, rows // 8 * CV + rows % 8, -1)
+    row_hot[...] = jnp.where(spot == ids, 1.0, 0.0).astype(bf16)
 
     running[0] = jnp.zeros(running.shape[1:], f32)
     for k in range(GROUP):
@@ -346,19 +359,10 @@
         NT, preferred_element_type=f32,
     )
     local = local * (1.0 / math.sqrt(FX * FY * dofs))
-    ids = ids_ref[...]
-    width = dense.shape[1]
-    spots = lax.broadcasted_iota(jnp.int32, (width, columns), 0)
-    one_hot = jnp.where(spots == ids, 1.0, 0.0).astype(f32)
-    rows = lax.broadcasted_iota(jnp.int32, (8 * subs, columns), 0)
-    spot = jnp.where(rows % 8 < CV, rows // 8 * CV + rows % 8, -1)
-    row_hot = jnp.where(spot == ids, 1.0, 0.0).astype(f32)
     placed = lax.dot_general(
-        local, one_hot, NT, precision=lax.Precision.HIGHEST, preferred_element_type=f32
-    )
-    dense[...] = jnp.dot(
-        row_hot, placed, precision=lax.Precision.HIGHEST, preferred_element_type=f32
-    )
+        two_parts(local, 1), one_hot[...], NT, preferred_element_type=f32
+    )
+    dense[...] = jnp.dot(row_hot[...], two_parts(placed, 0), preferred_element_type=f32)
 
     def block(s):
         return dense.at[pl.ds(pl.multiple_of(s * 8, 8), 8)]
@@ -493,6 +497,8 @@
             block(4, 2),
             block(2, FY),
             block(2, FX),
+            pltpu.VMEM((width, 2 * columns), bf16),
+            pltpu.VMEM((8 * subs, 2 * columns), bf16),
             pltpu.VMEM((8 * subs, width), f32),
             pltpu.VMEM((subs, 8, width), f32),
             pltpu.VMEM((8, width), f32),

time: 37.5 us -> 37 us (0.987)
  Pallas kernels: 27.4 us -> 26.6 us
    pallas_call x1, Pallas kernels: 27.4 us -> 26.6 us  [body(): pl.pallas_call(functools.partial(kernel, subs, slabs, slots, dofs), out_s...]
where the time goes in v5:
time: 37 us; the launch traced here: 36.3 us
  Pallas kernels  26.6 us (72%)
  local copies, waits for them, and re-layouts  8.33 us (23%)
  between operations  1.37 us (4%)
    pallas_call x1, Pallas kernels, body(): pl.pallas_call(functools.partial(kernel, subs, slabs, slots, dofs), out_s...  26.6 us
    reshape x1, local copies, waits for them, and re-layouts, body(): jac = jacobians.reshape(TYPES, 6, dofs, 6 * dofs)  3.1 us
    reshape x2, local copies, waits for them, and re-layouts, body(): x = coarse_basis.reshape(FX * FY, dofs, columns).transpose(0, 2, 1)  2.23 us
    reshape x1, local copies, waits for them, and re-layouts, body(): out = out[:, :, :dofs].transpose(0, 2, 1).reshape(FX, FY, dofs * columns)  1.82 us

profile of v5, /device:TPU:1, one launch (start us, length us, event | category | flops | bytes accessed | tf_op | source)
XLA Modules:
  0.0 36.3 jit_solution(2724807675252792136)
XLA Ops:
  1.3 1.8 %reshape.16 = bf16[32,125,32]{2,1,0:T(8,128)(2,1)S(1)} reshape(bf16[4,8,4000]{2,1,0:T(8,128)(2,1)} %param.6) | data formatting | bytes 512000 | tf_op jit(solution)/shard_map/reshape | solution.py:456
  3.1 0.4 %copy.9 = bf16[32,125,32]{1,2,0:T(8,128)(2,1)S(1)} copy(bf16[32,125,32]{2,1,0:T(8,128)(2,1)S(1)} %reshape.16) | data formatting | bytes 512000 | tf_op jit(solution)/shard_map/reshape | solution.py:456
  3.5 0.1 pad.4.x_ref
  3.6 0.0 copy-start
  3.6 0.0 copy-start.1
  3.6 0.0 copy-start.2
  3.6 3.1 %copy.12.jac_ref = bf16[4,6,125,750]{3,2,1,0:T(8,128)(2,1)S(1)} copy(bf16[4,6,125,750]{3,0,2,1:T(4,128)(2,1)} %bitcast.8) | data formatting | bytes 9000000 | tf_op jit(solution)/shard_map/reshape | solution.py:459
  6.7 0.0 copy-done
  6.7 0.0 copy-done.1
  6.8 0.0 copy-done.2
  6.8 26.6 %shard_map.77 = (bf16[32,32,128]{2,1,0:T(8,128)(2,1)S(1)}, f32[8,128]{1,0:T(8,128)S(1)}) custom-call(bf16[32,32,128]{2,1,0:T(8,128)(2,1)S(1)} %pad.4.x_ref, bf16[4,6,125,750]{3,2,1,0:T(8,128)(2,1)S(1)} %copy.12.jac_ref, s32[6,20]{1,0:T(8,128)S(1)} %bitcast.6, s32[1,20]{1,0:T(1,128)S(1)} %bitcast.7, s32[1]{0:T(128)S(6)} %copy.13.count_ref, s32[1,32]{1,0:T(1,128)S(1)} %copy-done.2), custom_call_target="tpu_custom_call" | custom-call | flops 1440000000 | bytes 4500000 | tf_op jit(solution)/shard_map/pallas_call | solution.py:466
  33.4 0.6 %slice.7 = f32[4,32]{1,0:T(4,128)} slice(f32[8,128]{1,0:T(8,128)S(1)} %get-tuple-element.5), slice={[0:4], [0:32]} | slice | bytes 1024 | tf_op jit(solution)/shard_map/slice | solution.py:523
  34.0 0.5 %copy.11 = bf16[32,125,32]{2,1,0:T(8,128)(2,1)S(1)} copy(bf16[32,125,32]{1,2,0:T(8,128)(2,1)S(1)} %slice_bitcast_fusion) | data formatting | bytes 512000 | tf_op jit(solution)/shard_map/transpose | solution.py:522
  34.5 1.8 %reshape.19 = bf16[4,8,4000]{2,1,0:T(8,128)(2,1)} reshape(bf16[32,125,32]{2,1,0:T(8,128)(2,1)S(1)} %copy.11) | data formatting | bytes 512000 | tf_op jit(solution)/shard_map/reshape | solution.py:522
  (1 shorter events, 0.0 us)
Async XLA Ops:
  3.6 3.2 %copy-start = (s32[20,6]{0,1:T(8,128)S(1)}, s32[20,6]{0,1:T(8,128)}, u32[]{:S(2)}) copy-start(s32[20,6]{0,1:T(8,128)} %param.8) | copy-start | bytes 1444
  3.6 3.1 %copy-start.1 = (s32[20]{0:T(128)S(1)}, s32[20]{0:T(128)}, u32[]{:S(2)}) copy-start(s32[20]{0:T(128)} %param.9) | copy-start | bytes 244
  3.6 3.1 %copy-start.2 = (s32[1,32]{1,0:T(1,128)S(1)}, s32[1,32]{1,0:T(1,128)}, u32[]{:S(2)}) copy-start(s32[1,32]{1,0:T(1,128)} %ids_ref.1) | copy-start | bytes 388

commit v6 on v5

--- a/solution.py
+++ b/solution.py
@@ -99,11 +99,71 @@
     return jnp.concatenate([high, rest], axis=axis)
 
 
+def columns_first(basis_ref, turned, flat):
+    f32 = jnp.float32
+    cells, columns = FX * FY, flat.shape[0] // (FX * FY)
+    length = basis_ref.shape[2]
+    per = LANES // columns
+    parts = LANES // cells
+    steps = LANES // (per * parts)
+    for n in range(steps):
+        blocks = []
+        for q in range(parts):
+            low = (q * steps + n) * LANES
+            high = min(low + LANES, length)
+            block = jnp.concatenate(
+                [basis_ref[r, :, low:high].astype(f32) for r in range(FX)], axis=0
+            )
+            if high - low < LANES:
+                end = jnp.zeros((cells, LANES - (high - low)), f32)
+                block = jnp.concatenate([block, end], axis=1)
+            blocks.append(block)
+        turned[n * LANES : (n + 1) * LANES, :] = jnp.concatenate(blocks, axis=0).T
+    for n in range(columns // per):
+        rows = [turned[pl.ds(n * per + k, LANES // per, stride=columns), :] for k in range(per)]
+        block = jnp.concatenate(rows, axis=0).T
+        for k in range(per):
+            lanes = slice(k * (LANES // per), (k + 1) * (LANES // per))
+            flat[pl.ds(n * per + k, cells, stride=columns), :] = jnp.concatenate(
+                [block[q * cells : (q + 1) * cells, lanes] for q in range(parts)], axis=1
+            )
+
+
+def dofs_first(flat, turned, out_ref):
+    cells, columns = FX * FY, flat.shape[0] // (FX * FY)
+    length = out_ref.shape[2]
+    per = LANES // columns
+    parts = LANES // cells
+    steps = LANES // (per * parts)
+    span = LANES // parts
+    for n in range(columns // per):
+        rows = [flat[pl.ds(n * per + k, cells, stride=columns), :] for k in range(per)]
+        block = jnp.concatenate(
+            [
+                jnp.concatenate([row[:, q * span : (q + 1) * span] for row in rows], axis=1)
+                for q in range(parts)
+            ],
+            axis=0,
+        ).T
+        for k in range(per):
+            turned[pl.ds(n * per + k, LANES // per, stride=columns), :] = block[
+                k * (LANES // per) : (k + 1) * (LANES // per)
+            ]
+    for n in range(steps):
+        block = turned[n * LANES : (n + 1) * LANES, :].T
+        for q in range(parts):
+            low = (q * steps + n) * LANES
+            high = min(low + LANES, length)
+            for r in range(FX):
+                top = q * cells + r * FY
+                out_ref[r, :, low:high] = block[top : top + FY, : high - low].astype(out_ref.dtype)
+
+
 def kernel(
     subs, slabs, slots, dofs,
-    x_ref, jac_ref, faces_ref, kinds_ref, count_ref, ids_ref,
+    basis_ref, jac_ref, faces_ref, kinds_ref, count_ref, ids_ref,
     out_ref, coarse_ref,
-    field, lists, meta_ref, jac, stacked, pieces, running, totals, sent, sent_cols, sent_diag, sent_cols_2,
+    x_ref, turned, flat, field, lists, meta_ref, jac, stacked, pieces, running, totals, sent, sent_cols, sent_diag, sent_cols_2,
     rim_cols, got_rows, got_cols, got_diag, got_rows_2, got_cols_2,
     one_hot, row_hot, dense, got_dense, row_sum, got_sum,
     list_sem, s0, r0, s1, r1, s2, r2, cs1, cr1, cs2, cr2,
@@ -180,9 +240,13 @@
     for k in range(4):
         fill(from_diagonals[k], got_diag.at[k])
 
+    columns_first(basis_ref, turned, flat)
     for r in range(FX):
         for c in range(FY):
-            field[cell(r + 1, c + 1)] = x_ref[r * FY + c]
+            k = r * FY + c
+            block = flat[k * columns : (k + 1) * columns, :].astype(bf16)
+            x_ref[k] = block
+            field[cell(r + 1, c + 1)] = block
 
     vertical = up.astype(jnp.int32) + down.astype(jnp.int32)
     sideways = left.astype(jnp.int32) + right.astype(jnp.int32)
@@ -423,7 +487,9 @@
                 v = v + wide(got_cols_2, 0, r - 1)
             if c == FY:
                 v = v + wide(got_cols_2, 1, r - 1)
-            out_ref[(r - 1) * FY + c - 1] = v.astype(bf16)
+            top = ((r - 1) * FY + c - 1) * columns
+            flat[top : top + columns, :] = v
+    dofs_first(flat, turned, out_ref)
 
     coarse_ref[...] = row_sum[...]
 
@@ -453,8 +519,6 @@
     width = -(-vertex_total // LANES) * LANES
     f32, bf16 = jnp.float32, jnp.bfloat16
 
-    x = coarse_basis.reshape(FX * FY, dofs, columns).transpose(0, 2, 1)
-    x = jnp.pad(x, ((0, 0), (0, 0), (0, LANES - dofs)))
     groups = group_count(slots)
     jac = jacobians.reshape(TYPES, 6, dofs, 6 * dofs)
 
@@ -466,7 +530,7 @@
     out, coarse = pl.pallas_call(
         functools.partial(kernel, subs, slabs, slots, dofs),
         out_shape=(
-            jax.ShapeDtypeStruct((FX * FY, columns, LANES), bf16),
+            jax.ShapeDtypeStruct(coarse_basis.shape, bf16),
             jax.ShapeDtypeStruct((8, width), f32),
         ),
         in_specs=[
@@ -479,6 +543,9 @@
         ],
         out_specs=(vmem, vmem),
         scratch_shapes=[
+            block(FX * FY),
+            pltpu.VMEM((columns * LANES // (LANES // (FX * FY)), LANES), f32),
+            pltpu.VMEM((FX * FY * columns, LANES), f32),
             block(CELLS),
             pltpu.VMEM((6 * slots, LANES), jnp.int32),
             pltpu.SMEM((6 * slots, LANES), jnp.int32),
@@ -518,8 +585,7 @@
             bytes_accessed=2 * jacobians.size,
             transcendentals=0,
         ),
-    )(x, jac, element_faces.T, element_type.reshape(1, slots), element_count, vertex_ids)
-    out = out[:, :, :dofs].transpose(0, 2, 1).reshape(FX, FY, dofs * columns)
+    )(coarse_basis, jac, element_faces.T, element_type.reshape(1, slots), element_count, vertex_ids)
     return out, coarse[:CV, :vertex_total]
 
 

time: 37 us -> 33.4 us (0.903); the launches traced: 36.3 us -> 33.4 us
  local copies, waits for them, and re-layouts: 8.33 us -> 4.4 us
  Pallas kernels: 26.6 us -> 27.6 us
    reshape x3 -> x0, local copies, waits for them, and re-layouts: 4.05 us -> none  [the longest x2 2.23 us: body(): x = coarse_basis.reshape(FX * FY, dofs, columns).transpose(0, 2, 1)]
    pallas_call x1, Pallas kernels: 26.6 us -> 27.6 us  [body(): pl.pallas_call(functools.partial(kernel, subs, slabs, slots, dofs), out_s...]
    unnamed x6 -> x9, local copies, waits for them, and re-layouts: 0.02 us -> 0.72 us
    transpose x2 -> x0, local copies, waits for them, and re-layouts: 0.52 us -> none  [body(): out = out[:, :, :dofs].transpose(0, 2, 1).reshape(FX, FY, dofs * columns)]
where the time goes in v6:
time: 33.4 us
  Pallas kernels  27.6 us (83%)
  local copies, waits for them, and re-layouts  4.4 us (13%)
  between operations  1.4 us (4%)
    pallas_call x1, Pallas kernels, body(): pl.pallas_call(functools.partial(kernel, subs, slabs, slots, dofs), out_s...  27.6 us
    reshape x1, local copies, waits for them, and re-layouts, body(): jac = jacobians.reshape(TYPES, 6, dofs, 6 * dofs)  3.1 us
    unnamed x9, local copies, waits for them, and re-layouts  0.72 us

profile of v6, /device:TPU:1, one launch (start us, length us, event | category | flops | bytes accessed | tf_op | source)
XLA Modules:
  0.0 33.4 jit_solution(18243873125175640433)
XLA Ops:
  0.6 0.0 copy-start.3
  0.6 0.0 copy-start.2
  0.7 0.0 copy-start.1
  0.7 0.0 copy-start
  1.4 3.1 %copy.10.jac_ref = bf16[4,6,125,750]{3,2,1,0:T(8,128)(2,1)S(1)} copy(bf16[4,6,125,750]{3,0,2,1:T(4,128)(2,1)} %bitcast.5) | data formatting | bytes 9000000 | tf_op jit(solution)/shard_map/reshape | solution.py:523
  4.5 0.0 copy-done.3
  4.5 0.0 copy-done.2
  4.5 0.0 copy-done.1
  4.5 0.0 copy-done
  4.5 27.6 %shard_map.77 = (bf16[4,8,4000]{2,1,0:T(8,128)(2,1)S(1)}, f32[8,128]{1,0:T(8,128)S(1)}) custom-call(bf16[4,8,4000]{2,1,0:T(8,128)(2,1)S(1)} %copy-done, bf16[4,6,125,750]{3,2,1,0:T(8,128)(2,1)S(1)} %copy.10.jac_ref, s32[6,20]{1,0:T(8,128)S(1)} %bitcast.3, s32[1,20]{1,0:T(1,128)S(1)} %bitcast.4, s32[1]{0:T(128)S(6)} %copy.12.count_ref, s32[1,32]{1,0:T(1,128)S(1)} %copy-done.3), custom_call_target="tpu_custom_call" | custom-call | flops 1440000000 | bytes 4500000 | tf_op jit(solution)/shard_map/pallas_call | solution.py:530
  32.1 0.6 %slice.3 = f32[4,32]{1,0:T(4,128)} slice(f32[8,128]{1,0:T(8,128)S(1)} %get-tuple-element.5), slice={[0:4], [0:32]} | slice | bytes 1024 | tf_op jit(solution)/shard_map/slice | solution.py:589
  32.6 0.7 %copy.13 = bf16[4,8,4000]{2,1,0:T(8,128)(2,1)} copy(bf16[4,8,4000]{2,1,0:T(8,128)(2,1)S(1)} %get-tuple-element.8) | data formatting | bytes 512000
Async XLA Ops:
  0.6 3.8 %copy-start.3 = (s32[1,32]{1,0:T(1,128)S(1)}, s32[1,32]{1,0:T(1,128)}, u32[]{:S(2)}) copy-start(s32[1,32]{1,0:T(1,128)} %ids_ref.1) | copy-start | bytes 388
  0.6 3.8 %copy-start.2 = (s32[20]{0:T(128)S(1)}, s32[20]{0:T(128)}, u32[]{:S(2)}) copy-start(s32[20]{0:T(128)} %param.9) | copy-start | bytes 244
  0.7 3.8 %copy-start.1 = (s32[20,6]{0,1:T(8,128)S(1)}, s32[20,6]{0,1:T(8,128)}, u32[]{:S(2)}) copy-start(s32[20,6]{0,1:T(8,128)} %param.8) | copy-start | bytes 1444
  0.7 3.8 %copy-start = (bf16[4,8,4000]{2,1,0:T(8,128)(2,1)S(1)}, bf16[4,8,4000]{2,1,0:T(8,128)(2,1)}, u32[]{:S(2)}) copy-start(bf16[4,8,4000]{2,1,0:T(8,128)(2,1)} %basis_ref.1) | copy-start | bytes 768004

commit v7 on v6

--- a/solution.py
+++ b/solution.py
@@ -161,12 +161,12 @@
 
 def kernel(
     subs, slabs, slots, dofs,
-    basis_ref, jac_ref, faces_ref, kinds_ref, count_ref, ids_ref,
+    basis_ref, jac_hbm, faces_ref, kinds_ref, count_ref, ids_ref,
     out_ref, coarse_ref,
-    x_ref, turned, flat, field, lists, meta_ref, jac, stacked, pieces, running, totals, sent, sent_cols, sent_diag, sent_cols_2,
+    x_ref, turned, flat, field, lists, meta_ref, raw, jac, stacked, pieces, running, totals, sent, sent_cols, sent_diag, sent_cols_2,
     rim_cols, got_rows, got_cols, got_diag, got_rows_2, got_cols_2,
     one_hot, row_hot, dense, got_dense, row_sum, got_sum,
-    list_sem, s0, r0, s1, r1, s2, r2, cs1, cr1, cs2, cr2,
+    list_sem, jac_sem, s0, r0, s1, r1, s2, r2, cs1, cr1, cs2, cr2,
 ):
     i = lax.axis_index("sub")
     j = lax.axis_index("slab")
@@ -174,6 +174,15 @@
     columns = x_ref.shape[1]
     f32 = jnp.float32
     bf16 = jnp.bfloat16
+
+    jac_copies = [
+        pltpu.make_async_copy(
+            jac_hbm.at[pl.ds(p * dofs, dofs)], raw.at[pl.ds(p * dofs, dofs)], jac_sem.at[p]
+        )
+        for p in range(6)
+    ]
+    for copy in jac_copies:
+        copy.start()
 
     barrier = pltpu.get_barrier_semaphore()
 
@@ -287,18 +296,21 @@
     )
     exchange(first)
 
-    @pl.loop(0, TYPES * 6)
-    def _(n):
-        t, r = n // 6, n % 6
+    for copy in jac_copies:
+        copy.wait()
+
+    @pl.loop(0, 6)
+    def _(r):
         top = pl.multiple_of(r * LANES, LANES)
-        face_rows = jac_ref[t, r]
-        end = jnp.zeros((dofs, LANES - dofs), bf16)
-        for p in range(6):
-            lanes = slice(p * LANES, (p + 1) * LANES)
-            jac[t, pl.ds(top + LANES - 16, 16), lanes] = jnp.zeros((16, LANES), bf16)
-            jac[t, pl.ds(top, dofs), lanes] = jnp.concatenate(
-                [face_rows[:, p * dofs : (p + 1) * dofs], end], axis=1
-            )
+        for t in range(TYPES):
+            face_rows = raw[pl.ds(r * dofs, dofs), t, :]
+            end = jnp.zeros((dofs, LANES - dofs), bf16)
+            for p in range(6):
+                lanes = slice(p * LANES, (p + 1) * LANES)
+                jac[t, pl.ds(top + LANES - 16, 16), lanes] = jnp.zeros((16, LANES), bf16)
+                jac[t, pl.ds(top, dofs), lanes] = jnp.concatenate(
+                    [face_rows[:, p * dofs : (p + 1) * dofs], end], axis=1
+                )
 
     list_copy.wait()
     arrive(first)
@@ -520,7 +532,7 @@
     f32, bf16 = jnp.float32, jnp.bfloat16
 
     groups = group_count(slots)
-    jac = jacobians.reshape(TYPES, 6, dofs, 6 * dofs)
+    jac = jacobians.transpose(1, 0, 2)
 
     def block(*lead):
         return pltpu.VMEM((*lead, columns, LANES), bf16)
@@ -535,7 +547,7 @@
         ),
         in_specs=[
             vmem,
-            vmem,
+            pl.BlockSpec(memory_space=pl.ANY),
             vmem,
             vmem,
             pl.BlockSpec(memory_space=pltpu.SMEM),
@@ -549,6 +561,7 @@
             block(CELLS),
             pltpu.VMEM((6 * slots, LANES), jnp.int32),
             pltpu.SMEM((6 * slots, LANES), jnp.int32),
+            pltpu.VMEM((6 * dofs, TYPES, 6 * dofs), bf16),
             pltpu.VMEM((TYPES, 6 * LANES, 6 * LANES), bf16),
             pltpu.VMEM((slots + GROUP, columns, 6 * LANES), bf16),
             pltpu.VMEM((6 * GROUP * groups, columns, LANES), f32),
@@ -570,7 +583,7 @@
             pltpu.VMEM((subs, 8, width), f32),
             pltpu.VMEM((8, width), f32),
             pltpu.VMEM((slabs, 8, width), f32),
-            dma,
+            dma, dma((6,)),
             dma((4,)), dma((4,)),
             dma((8,)), dma((8,)),
             dma((4,)), dma((4,)),

time: 33.4 us -> 45.3 us (1.36)
  Pallas kernels: 27.6 us -> 37.2 us
  local copies, waits for them, and re-layouts: 4.4 us -> 6.53 us
    pallas_call x1, Pallas kernels: 27.6 us -> 37.2 us  [body(): pl.pallas_call(functools.partial(kernel, subs, slabs, slots, dofs), out_s...]
    unnamed x9 -> x11, local copies, waits for them, and re-layouts: 0.72 us -> 5.95 us
    reshape x1 -> x0, local copies, waits for them, and re-layouts: 3.1 us -> none  [body(): jac = jacobians.reshape(TYPES, 6, dofs, 6 * dofs)]
where the time goes in v7:
time: 45.3 us; the launch traced here: 45.1 us
  Pallas kernels  37.2 us (82%)
  local copies, waits for them, and re-layouts  6.53 us (14%)
  between operations  1.3 us (3%)
    pallas_call x1, Pallas kernels, body(): pl.pallas_call(functools.partial(kernel, subs, slabs, slots, dofs), out_s...  37.2 us
    unnamed x11, local copies, waits for them, and re-layouts  5.95 us

profile of v7, /device:TPU:1, one launch (start us, length us, event | category | flops | bytes accessed | tf_op | source)
XLA Modules:
  0.0 45.1 jit_solution(1144637497469539154)
XLA Ops:
  1.3 0.0 copy-start
  1.3 2.3 %copy-done = bf16[4,750,750]{2,0,1:T(4,128)(2,1)S(1)} copy-done((bf16[4,750,750]{2,0,1:T(4,128)(2,1)S(1)}, bf16[4,750,750]{2,0,1:T(4,128)(2,1)}, u32[]{:S(2)}) %copy-start) | copy-done | bytes 4500024
  3.6 0.0 copy-start.1
  3.6 0.9 %copy-done.1 = bf16[4,8,4000]{2,1,0:T(8,128)(2,1)S(1)} copy-done((bf16[4,8,4000]{2,1,0:T(8,128)(2,1)S(1)}, bf16[4,8,4000]{2,1,0:T(8,128)(2,1)}, u32[]{:S(2)}) %copy-start.1) | copy-done | bytes 256024
  4.5 0.0 copy-start.2
  4.5 0.7 %copy-done.2 = s32[20,6]{0,1:T(8,128)S(1)} copy-done((s32[20,6]{0,1:T(8,128)S(1)}, s32[20,6]{0,1:T(8,128)}, u32[]{:S(2)}) %copy-start.2) | copy-done | bytes 504
  5.2 0.0 copy-start.3
  5.2 0.7 %copy-done.3 = s32[20]{0:T(128)S(1)} copy-done((s32[20]{0:T(128)S(1)}, s32[20]{0:T(128)}, u32[]{:S(2)}) %copy-start.3) | copy-done | bytes 104
  5.9 0.0 copy-start.4
  5.9 0.7 %copy-done.4 = s32[1,32]{1,0:T(1,128)S(1)} copy-done((s32[1,32]{1,0:T(1,128)S(1)}, s32[1,32]{1,0:T(1,128)}, u32[]{:S(2)}) %copy-start.4) | copy-done | bytes 152
  6.5 37.2 %shard_map.77 = (bf16[4,8,4000]{2,1,0:T(8,128)(2,1)S(1)}, f32[8,128]{1,0:T(8,128)S(1)}) custom-call(bf16[4,8,4000]{2,1,0:T(8,128)(2,1)S(1)} %copy-done.1, bf16[750,4,750]{2,1,0:T(4,128)(2,1)S(1)} %bitcast.3, s32[6,20]{1,0:T(8,128)S(1)} %bitcast.4, s32[1,20]{1,0:T(1,128)S(1)} %bitcast.5, s32[1]{0:T(128)S(6)} %copy.9.count_ref, s32[1,32]{1,0:T(1,128)S(1)} %copy-done.4), custom_call_target="tpu_custom_call" | custom-call | flops 1440000000 | bytes 4500000 | tf_op jit(solution)/shard_map/pallas_call | solution.py:542
  43.8 0.6 %slice.3 = f32[4,32]{1,0:T(4,128)} slice(f32[8,128]{1,0:T(8,128)S(1)} %get-tuple-element.5), slice={[0:4], [0:32]} | slice | bytes 1024 | tf_op jit(solution)/shard_map/slice | solution.py:602
  44.4 0.7 %copy.10 = bf16[4,8,4000]{2,1,0:T(8,128)(2,1)} copy(bf16[4,8,4000]{2,1,0:T(8,128)(2,1)S(1)} %get-tuple-element.8) | data formatting | bytes 512000
Async XLA Ops:
  1.3 2.3 %copy-start = (bf16[4,750,750]{2,0,1:T(4,128)(2,1)S(1)}, bf16[4,750,750]{2,0,1:T(4,128)(2,1)}, u32[]{:S(2)}) copy-start(bf16[4,750,750]{2,0,1:T(4,128)(2,1)} %param.7) | copy-start | bytes 13500004
  3.6 0.9 %copy-start.1 = (bf16[4,8,4000]{2,1,0:T(8,128)(2,1)S(1)}, bf16[4,8,4000]{2,1,0:T(8,128)(2,1)}, u32[]{:S(2)}) copy-start(bf16[4,8,4000]{2,1,0:T(8,128)(2,1)} %basis_ref.1) | copy-start | bytes 768004
  4.5 0.7 %copy-start.2 = (s32[20,6]{0,1:T(8,128)S(1)}, s32[20,6]{0,1:T(8,128)}, u32[]{:S(2)}) copy-start(s32[20,6]{0,1:T(8,128)} %param.8) | copy-start | bytes 1444
  5.2 0.7 %copy-start.3 = (s32[20]{0:T(128)S(1)}, s32[20]{0:T(128)}, u32[]{:S(2)}) copy-start(s32[20]{0:T(128)} %param.9) | copy-start | bytes 244
  5.9 0.7 %copy-start.4 = (s32[1,32]{1,0:T(1,128)S(1)}, s32[1,32]{1,0:T(1,128)}, u32[]{:S(2)}) copy-start(s32[1,32]{1,0:T(1,128)} %ids_ref.1) | copy-start | bytes 388

commit v8 on v6

--- a/solution.py
+++ b/solution.py
@@ -17,10 +17,10 @@
 TYPES = 4
 LANES = 128
 GROUP = 4
-GATHER = 4
+GATHER = 10
 TOGETHER = 4
-SUMS = 8
-SPREAD = 4
+SUMS = 20
+SPREAD = 10
 MESH = pl.DeviceIdType.MESH
 NT = (((1,), (1,)), ((), ()))
 
@@ -201,10 +201,6 @@
         def _():
             greet(di, dj)
 
-    index_lists(faces_ref, kinds_ref, count_ref[0], lists)
-    list_copy = pltpu.make_async_copy(lists, meta_ref, list_sem)
-    list_copy.start()
-
     ids = jnp.concatenate([ids_ref[...]] * 2, axis=1)
     spots = lax.broadcasted_iota(jnp.int32, one_hot.shape, 0)
     one_hot[...] = jnp.where(spots == ids, 1.0, 0.0).astype(bf16)
@@ -286,6 +282,10 @@
         (right, left, remote(x_cols.at[:, FY - 1], rim_cols.at[0], s0.at[3], r0.at[3], i, j + 1)),
     )
     exchange(first)
+    index_lists(faces_ref, kinds_ref, count_ref[0], lists)
+    list_copy = pltpu.make_async_copy(lists, meta_ref, list_sem)
+    list_copy.start()
+
 
     @pl.loop(0, TYPES * 6)
     def _(n):

time: 33.4 us -> 33.5 us (level)
  no operation moved by 1% of the time
where the time goes in v8:
time: 33.5 us; the launch traced here: 33.4 us
  Pallas kernels  27.6 us (82%)
  local copies, waits for them, and re-layouts  4.4 us (13%)
  between operations  1.4 us (4%)
    pallas_call x1, Pallas kernels, body(): pl.pallas_call(functools.partial(kernel, subs, slabs, slots, dofs), out_s...  27.6 us
    reshape x1, local copies, waits for them, and re-layouts, body(): jac = jacobians.reshape(TYPES, 6, dofs, 6 * dofs)  3.1 us
    unnamed x9, local copies, waits for them, and re-layouts  0.72 us

profile of v8, /device:TPU:1, one launch (start us, length us, event | category | flops | bytes accessed | tf_op | source)
XLA Modules:
  0.0 33.4 jit_solution(16599309411895022449)
XLA Ops:
  0.6 0.0 copy-start.3
  0.6 0.0 copy-start.2
  0.7 0.0 copy-start.1
  0.7 0.0 copy-start
  1.4 3.1 %copy.10.jac_ref = bf16[4,6,125,750]{3,2,1,0:T(8,128)(2,1)S(1)} copy(bf16[4,6,125,750]{3,0,2,1:T(4,128)(2,1)} %bitcast.5) | data formatting | bytes 9000000 | tf_op jit(solution)/shard_map/reshape | solution.py:523
  4.5 0.0 copy-done.3
  4.5 0.0 copy-done.2
  4.5 0.0 copy-done.1
  4.5 0.0 copy-done
  4.5 27.6 %shard_map.77 = (bf16[4,8,4000]{2,1,0:T(8,128)(2,1)S(1)}, f32[8,128]{1,0:T(8,128)S(1)}) custom-call(bf16[4,8,4000]{2,1,0:T(8,128)(2,1)S(1)} %copy-done, bf16[4,6,125,750]{3,2,1,0:T(8,128)(2,1)S(1)} %copy.10.jac_ref, s32[6,20]{1,0:T(8,128)S(1)} %bitcast.3, s32[1,20]{1,0:T(1,128)S(1)} %bitcast.4, s32[1]{0:T(128)S(6)} %copy.12.count_ref, s32[1,32]{1,0:T(1,128)S(1)} %copy-done.3), custom_call_target="tpu_custom_call" | custom-call | flops 1440000000 | bytes 4500000 | tf_op jit(solution)/shard_map/pallas_call | solution.py:530
  32.1 0.6 %slice.3 = f32[4,32]{1,0:T(4,128)} slice(f32[8,128]{1,0:T(8,128)S(1)} %get-tuple-element.5), slice={[0:4], [0:32]} | slice | bytes 1024 | tf_op jit(solution)/shard_map/slice | solution.py:589
  32.7 0.7 %copy.13 = bf16[4,8,4000]{2,1,0:T(8,128)(2,1)} copy(bf16[4,8,4000]{2,1,0:T(8,128)(2,1)S(1)} %get-tuple-element.8) | data formatting | bytes 512000
Async XLA Ops:
  0.6 3.8 %copy-start.3 = (s32[1,32]{1,0:T(1,128)S(1)}, s32[1,32]{1,0:T(1,128)}, u32[]{:S(2)}) copy-start(s32[1,32]{1,0:T(1,128)} %ids_ref.1) | copy-start | bytes 388
  0.6 3.8 %copy-start.2 = (s32[20]{0:T(128)S(1)}, s32[20]{0:T(128)}, u32[]{:S(2)}) copy-start(s32[20]{0:T(128)} %param.9) | copy-start | bytes 244
  0.7 3.8 %copy-start.1 = (s32[20,6]{0,1:T(8,128)S(1)}, s32[20,6]{0,1:T(8,128)}, u32[]{:S(2)}) copy-start(s32[20,6]{0,1:T(8,128)} %param.8) | copy-start | bytes 1444
  0.7 3.8 %copy-start = (bf16[4,8,4000]{2,1,0:T(8,128)(2,1)S(1)}, bf16[4,8,4000]{2,1,0:T(8,128)(2,1)}, u32[]{:S(2)}) copy-start(bf16[4,8,4000]{2,1,0:T(8,128)(2,1)} %basis_ref.1) | copy-start | bytes 768004
